TPU v7x, 128 devices: a whole 4x4x4 slice. The times are simulated.
128 devices in a mesh: fsdp: 16 (over x, y), replica: 8 (over z, core).
Axes of the slice: x: 4, y: 4, z: 4, core: 2. Of those that a mesh axis runs over, the one named last changes fastest.
Arguments:
- grads: bfloat16 [8, 6144, 6144], P('replica', 'fsdp'), may hold values from -80 to 80
- errors: bfloat16 [8, 6144, 6144], P('replica', 'fsdp'), may hold values from -1.25 to 1.25
- q_start: float32 [6144, 128], P('fsdp'), may hold values from -0.078125 to 0.078125
- clip_rms: float32 [], replicated, may hold values from 1.5 to 2.5
Outputs:
- new_errors: bfloat16 [8, 6144, 6144], P('replica', 'fsdp')
- p_basis: float32 [6144, 128], P('fsdp')
- q_out: float32 [6144, 128], P('fsdp')
All inputs are finite; a program needn't handle non-finite values.
Results may differ from a plain program's by a relative error of at most 0.02.
Values may be sent and summed in bfloat16 or wider, within the bound.
A program may use at most 64 MiB of HBM per device.

v0:
```python
import jax
import jax.numpy as jnp
from jax import lax
from jax.sharding import PartitionSpec as P


def body(grads, errors, q_start, clip_rms):
    merged = grads[0].astype(jnp.float32) + errors[0].astype(jnp.float32)
    squares = jnp.sum(merged * merged)
    merged_b = merged.astype(jnp.bfloat16)
    col_count = merged_b.shape[1]
    replicas = lax.axis_size("replica")
    columns = merged_b
    p_local = jnp.dot(
        columns,
        lax.all_gather(q_start.astype(jnp.bfloat16), "fsdp", axis=0, tiled=True),
        preferred_element_type=jnp.float32,
    )
    p_sum = lax.psum(p_local, "replica")
    gram_part = lax.dot_general(
        p_sum, p_sum, (((0,), (0,)), ((), ())), precision=lax.Precision.HIGHEST
    )
    gram = lax.psum(gram_part.astype(jnp.bfloat16), "fsdp").astype(jnp.float32)
    square_all = lax.psum(squares, ("fsdp", "replica"))
    factor = jnp.linalg.cholesky(gram)
    p_basis = jax.scipy.linalg.solve_triangular(factor, p_sum.T, lower=True).T
    p_low = p_basis.astype(jnp.bfloat16)
    columns = merged_b
    q_part = lax.psum_scatter(
        lax.dot_general(
            columns, p_low, (((0,), (0,)), ((), ())), preferred_element_type=jnp.float32
        ).astype(jnp.bfloat16),
        "fsdp",
        scatter_dimension=0,
        tiled=True,
    )
    q_mean = lax.psum(q_part, "replica").astype(jnp.float32) / replicas
    columns = merged_b
    update = lax.dot_general(
        p_low,
        lax.all_gather(q_mean.astype(jnp.bfloat16), "fsdp", axis=0, tiled=True),
        (((1,), (1,)), ((), ())),
        preferred_element_type=jnp.float32,
    )
    new_errors = (columns.astype(jnp.float32) - update).astype(jnp.bfloat16)
    root_mean = jnp.sqrt(square_all / (replicas * col_count * col_count) + 1e-06)
    clip_scale = jnp.minimum(jnp.float32(1.0), clip_rms / root_mean)
    return (new_errors[None], p_basis, clip_scale * q_mean)


def solution(mesh):
    return jax.shard_map(
        body,
        mesh=mesh,
        in_specs=(P("replica", "fsdp", None), P("replica", "fsdp", None), P("fsdp", None), P()),
        out_specs=(P("replica", "fsdp", None), P("fsdp", None), P("fsdp", None)),
        check_vma=False,
    )
```

profile of v0, /device:TPU:1, one launch (start us, length us, event | category | flops | bytes accessed | tf_op | source)
XLA Modules:
  0.0 426.5 jit_solution(1092664153934042494)
XLA Ops:
  7.2 0.0 all-gather.3.cloned.1.call-start
  7.2 1.6 convert_element_type.46
  8.8 0.0 all-gather.3.cloned.1.call-update
  8.8 0.0 all-reduce.3.cloned.1.call-start
  8.9 48.0 %all-gather.3.cloned.1.call-done = bf16[6144,128]{1,0:T(8,128)(2,1)} async-done(((bf16[384,128]{1,0:T(8,128)(2,1)}), bf16[6144,128]{1,0:T(8,128)(2,1)}) %all-gather.3.cloned.1.call-update) | async-done | bytes 1572880 | tf_op jit(solution)/shard_map/all_gather | solution.py:16
  56.9 6.2 %fusion.11 = f32[384,128]{1,0:T(8,128)} fusion(bf16[6144,128]{1,0:T(8,128)(2,1)} %all-gather.3.cloned.1.call-done, bf16[1,384,6144]{2,1,0:T(8,128)(2,1)} %param.5, bf16[1,384,6144]{2,1,0:T(8,128)(2,1)} %param.4), kind=kOutput, calls=%fused_computation.23 | convolution fusion | flops 613416960 | bytes 11206656 | tf_op jit(solution)/shard_map/dot_general | solution.py:14
  63.1 0.0 all-reduce.3.cloned.1.call-update
  63.1 0.0 reduce-scatter.2.cloned.1.call-start
  63.2 58.3 %all-reduce.3.cloned.1.call-done = f32[384,128]{1,0:T(8,128)} async-done(((f32[384,128]{1,0:T(8,128)}), f32[384,128]{1,0:T(8,128)}) %all-reduce.3.cloned.1.call-update) | async-done | bytes 196624 | tf_op jit(solution)/shard_map/psum | solution.py:19
  121.5 1.5 convolution_convert_fusion.1
  123.0 60.3 %psum.29 = bf16[128,128]{0,1:T(8,128)(2,1)S(1)} all-reduce(bf16[128,128]{0,1:T(8,128)(2,1)S(1)} %convolution_convert_fusion.1), channel_id=1, replica_groups=mesh['fsdp'=16,'replica'=8] {'fsdp'}, use_global_device_ids=true, to_apply=%region_1.0 | all-reduce | flops 16384 | bytes 65536 | tf_op jit(solution)/shard_map/psum | solution.py:23
  183.3 0.1 copy.8
  183.4 11.7 %cholesky.16 = f32[128,128]{1,0:T(8,128)S(1)} custom-call(f32[128,128]{1,0:T(8,128)S(1)} %fusion.7), custom_call_target="Cholesky" | custom-call | tf_op jit(solution)/shard_map/jit(cholesky)/cholesky | solution.py:25
  195.2 0.6 compare_reduce_fusion
  195.8 0.7 fusion.4
  196.5 9.8 %custom-call.7 = f32[1,128,128]{1,2,0:T(8,128)S(1)} custom-call(f32[1,128,128]{2,1,0:T(8,128)S(1)} %fusion.4), custom_call_target="InvertDiagBlocksLowerTriangular" | custom-call | tf_op jit(solution)/shard_map/jit(_solve_triangular)/triangular_solve | solution.py:26
  206.3 1.2 fusion.5
  207.5 0.0 copy-start
  207.6 6.9 %convolution_convert_fusion = bf16[6144,128]{1,0:T(8,128)(2,1)} fusion(f32[384,128]{1,0:T(8,128)S(1)} %fusion.5, bf16[1,384,6144]{2,1,0:T(8,128)(2,1)} %param.5, bf16[1,384,6144]{2,1,0:T(8,128)(2,1)} %param.4), kind=kOutput, calls=%fused_computation.5 | convolution fusion | flops 614252544 | bytes 11206656 | tf_op jit(solution)/shard_map/dot_general | solution.py:30
  214.4 0.0 reduce-scatter.2.cloned.1.call-update
  214.5 0.0 all-reduce.5.cloned.1.call-start
  214.5 81.8 %reduce-scatter.2.cloned.1.call-done = bf16[384,128]{1,0:T(8,128)(2,1)} async-done(((bf16[6144,128]{1,0:T(8,128)(2,1)}), bf16[384,128]{1,0:T(8,128)(2,1)}) %reduce-scatter.2.cloned.1.call-update) | async-done | bytes 98320 | tf_op jit(solution)/shard_map/reduce_scatter | solution.py:29
  296.3 0.0 all-reduce.5.cloned.1.call-update
  296.4 0.2 all-gather.5.cloned.1.call-start
  296.6 6.8 %multiply_reduce_fusion = f32[]{:T(128)} fusion(bf16[1,384,6144]{2,1,0:T(8,128)(2,1)} %param.5, bf16[1,384,6144]{2,1,0:T(8,128)(2,1)} %param.4), kind=kLoop, calls=%fused_computation | loop fusion | flops 11796479 | bytes 9437188 | tf_op jit(solution)/shard_map/reduce_sum | solution.py:9
  303.4 66.1 %psum.31 = f32[]{:T(128)} all-reduce(f32[]{:T(128)} %multiply_reduce_fusion), channel_id=1, replica_groups=mesh['fsdp'=16,'replica'=8] {'fsdp','replica'}, use_global_device_ids=true, to_apply=%region_7.8 | all-reduce | flops 1 | bytes 8 | tf_op jit(solution)/shard_map/psum | solution.py:24
  370.9 0.0 all-reduce.5.cloned.1.call-done
  370.9 1.6 convert_multiply_fusion
  372.5 0.0 all-gather.5.cloned.1.call-update
  372.6 39.5 %all-gather.5.cloned.1.call-done = bf16[6144,128]{1,0:T(8,128)(2,1)} async-done(((bf16[384,128]{1,0:T(8,128)(2,1)}), bf16[6144,128]{1,0:T(8,128)(2,1)}) %all-gather.5.cloned.1.call-update) | async-done | bytes 1572880 | tf_op jit(solution)/shard_map/all_gather | solution.py:41
  412.0 0.0 copy-done
  412.0 7.9 %fusion.1 = bf16[1,384,6144]{2,1,0:T(8,128)(2,1)} fusion(bf16[6144,128]{1,0:T(8,128)(2,1)} %all-gather.5.cloned.1.call-done, f32[384,128]{1,0:T(8,128)S(1)} %fusion.5, bf16[1,384,6144]{2,1,0:T(8,128)(2,1)} %param.5, bf16[1,384,6144]{2,1,0:T(8,128)(2,1)} %param.4), kind=kOutput, calls=%fused_computation.4 | convolution fusion | flops 620544000 | bytes 15925248 | tf_op jit(solution)/shard_map/dot_general | solution.py:39
  (2 shorter events, 0.0 us)
Async XLA Ops:
  7.2 49.7 %all-gather.3.cloned.1.call-start = ((), (), s32[]{:S(2)}) async-start(), calls=%async_computation.1 | async-start | bytes 1671168 | tf_op jit(solution)/shard_map/all_gather | solution.py:16
  8.8 112.7 %all-reduce.3.cloned.1.call-start = ((), (), s32[]{:S(2)}) async-start(), calls=%async_computation.2 | async-start | bytes 393216 | tf_op jit(solution)/shard_map/psum | solution.py:19
  63.1 233.2 %reduce-scatter.2.cloned.1.call-start = ((), (), s32[]{:S(2)}) async-start(), calls=%async_computation.3 | async-start | bytes 1671168 | tf_op jit(solution)/shard_map/reduce_scatter | solution.py:29
  207.5 204.5 %copy-start = (f32[384,128]{1,0:T(8,128)}, f32[384,128]{1,0:T(8,128)S(1)}, u32[]{:S(2)}) copy-start(f32[384,128]{1,0:T(8,128)S(1)} %fusion.5) | copy-start | bytes 589828
  214.5 156.4 %all-reduce.5.cloned.1.call-start = ((), (), s32[]{:S(2)}) async-start(), calls=%async_computation.4 | async-start | bytes 196608 | tf_op jit(solution)/shard_map/psum | solution.py:37
  296.4 115.7 %all-gather.5.cloned.1.call-start = ((), (), s32[]{:S(2)}) async-start(), calls=%async_computation.5 | async-start | bytes 1671168 | tf_op jit(solution)/shard_map/all_gather | solution.py:41
Sparse Core Ops, SparseCore 0:
  10.8 46.0 all-gather.2
  63.3 58.1 all-reduce.2
  214.6 81.6 reduce-scatter.1
  298.6 56.3 all-reduce.4
  372.7 39.3 all-gather.4
where the time goes:
time: 427 us; the launch traced here: 426 us
  waiting for transfers between devices  228 us (53%)
  blocking collectives  126 us (30%)
  other arithmetic  32.9 us (8%)
  matrix products  23.8 us (6%)
  between operations  15.2 us (4%)
    reduce_scatter x1, waiting for transfers between devices, body(): lax.psum_scatter(lax.dot_general(columns, p_low, (((0,), (0,)), ((), ()))...  81.8 us
    psum x1, blocking collectives, body(): square_all = lax.psum(squares, ('fsdp', 'replica'))  66.1 us
    psum x1, blocking collectives, body(): gram = lax.psum(gram_part.astype(jnp.bfloat16), 'fsdp').astype(jnp.float32)  60.3 us
    psum x1, waiting for transfers between devices, body(): p_sum = lax.psum(p_local, 'replica')  58.3 us
    all_gather x1, waiting for transfers between devices, body(): lax.all_gather(q_start.astype(jnp.bfloat16), 'fsdp', axis=0, tiled=True)  48 us
    all_gather x1, waiting for transfers between devices, body(): lax.all_gather(q_mean.astype(jnp.bfloat16), 'fsdp', axis=0, tiled=True)  39.5 us
    another operation x3, other arithmetic, body(): factor = jnp.linalg.cholesky(gram)  12.4 us
    another operation x2, other arithmetic, body(): p_basis = jax.scipy.linalg.solve_triangular(factor, p_sum.T, lower=True).T  10.5 us
  transfers between devices with their start and end apart: 5, of which 4 were waited for; matrix products, arithmetic and copies ran while one was open for 2% of the time, Pallas kernels for 0%

commit v1 on v0

v1 whole, which is shorter than its diff:
```python
import jax
import jax.numpy as jnp
from jax import lax
from jax.experimental import pallas as pl
from jax.experimental.pallas import tpu as pltpu
from jax.sharding import PartitionSpec as P

MESH = pl.DeviceIdType.MESH
F32 = jnp.float32
BF16 = jnp.bfloat16

ROWS = 384
D = 6144
RANK = 128
CHUNKS = 8
CHUNK = ROWS // CHUNKS
HALF = ROWS // 2
PIECE = ROWS // 8


def mod4(v):
    return lax.rem(v, 4)


def split3(v):
    a = v.astype(BF16).astype(F32)
    b = (v - a).astype(BF16).astype(F32)
    return a, b, (v - a - b).astype(BF16).astype(F32)


def tile_of(part, x, y, z):
    return (z * 16 + x * 4 + y, x * 16 + y * 4 + z, y * 16 + z * 4 + x)[part]


def exchange(
    clip_ref,
    grads,
    errors,
    q_ref,
    merged_out,
    yt_out,
    bmat_ref,
    basis_ref,
    w_ref,
    gbuf,
    ebuf,
    qh,
    pacc,
    sq,
    psend,
    precv,
    pall,
    pt,
    gsend,
    gxr,
    gyr,
    gmat,
    aug,
    wbuf,
    yl,
    yr,
    yc,
    rs1,
    rs2,
    rs3,
    t1,
    t2,
    gy,
    load_sem,
    out_sem,
    yt_sem,
    q1s,
    q1r,
    q2s,
    q2r,
    q3s,
    q3r,
    p1s,
    p1r,
    p2s,
    p2r,
    gxs,
    gxq,
    gys,
    gyq,
    gas,
    gaq,
    cs,
    cr,
    r1s,
    r1r,
    r2s,
    r2r,
    r3s,
    r3r,
    a1s,
    a1r,
    a2s,
    a2r,
    a3s,
    a3r,
    ss,
    sr,
):
    f = lax.axis_index("fsdp")
    r = lax.axis_index("replica")
    x, y, z, c = f // 4, lax.rem(f, 4), r // 2, lax.rem(r, 2)
    sibling = (f, z * 2 + 1 - c)

    def on_x(d):
        return (mod4(x + d) * 4 + y, r)

    def on_y(d):
        return (x * 4 + mod4(y + d), r)

    def on_z(d):
        return (f, mod4(z + d) * 2 + c)

    def send(src, dst, ssem, rsem, device):
        copy = pltpu.make_async_remote_copy(
            src_ref=src, dst_ref=dst, send_sem=ssem, recv_sem=rsem, device_id=device, device_id_type=MESH
        )
        copy.start()
        return copy

    sent = []

    loads = []
    for k in range(CHUNKS):
        rows = pl.ds(k * CHUNK, CHUNK)
        a = pltpu.make_async_copy(grads.at[rows], gbuf.at[rows], load_sem.at[0, k])
        b = pltpu.make_async_copy(errors.at[rows], ebuf.at[rows], load_sem.at[1, k])
        a.start()
        b.start()
        loads.append((a, b))

    s_me, t_me = jnp.where(c == 0, y, x), jnp.where(c == 0, x, y)
    qh[c, s_me, t_me] = q_ref[pl.ds(pl.multiple_of(c * HALF, HALF), HALF), :].astype(BF16)

    barrier = pltpu.get_barrier_semaphore()
    peers = [sibling]
    for d in (1, 2, 3):
        peers += [on_x(d), on_y(d), on_z(d), (f, mod4(z + d) * 2 + 1 - c)]
    for device in peers:
        pl.semaphore_signal(barrier, inc=1, device_id=device, device_id_type=MESH)
    pl.semaphore_wait(barrier, len(peers))

    def along(first, d):
        if first:
            return (jnp.where(c == 0, mod4(x + d) * 4 + y, x * 4 + mod4(y + d)), r)
        return (jnp.where(c == 0, x * 4 + mod4(y + d), mod4(x + d) * 4 + y), r)

    q1 = []
    for d in (1, 2, 3):
        here = qh.at[c, s_me, t_me]
        q1.append(send(here, here, q1s.at[d - 1], q1r.at[d - 1], along(True, d)))

    sq[...] = jnp.zeros_like(sq)

    def merge(k):
        a, b = loads[k]
        a.wait()
        b.wait()

        def group(i, _):
            rows = pl.ds(pl.multiple_of(k * CHUNK + i * 16, 16), 16)
            total = jnp.zeros((16, 128), F32)
            for j in range(D // 768):
                cols = pl.ds(j * 768, 768)
                m = gbuf[rows, cols].astype(F32) + ebuf[rows, cols].astype(F32)
                gbuf[rows, cols] = m.astype(BF16)
                m2 = m * m
                for i2 in range(6):
                    total = total + m2[:, i2 * 128 : (i2 + 1) * 128]
            sq[...] += total[:8] + total[8:]
            return 0

        lax.fori_loop(0, CHUNK // 16, group, 0)
        rows = pl.ds(k * CHUNK, CHUNK)
        out = pltpu.make_async_copy(gbuf.at[rows], merged_out.at[rows], out_sem.at[k])
        out.start()
        return out

    outs = [merge(0), merge(1)]
    for copy in q1:
        copy.wait_recv()
    q2 = []
    for d in (1, 2, 3):
        here = qh.at[c, s_me]
        q2.append(send(here, here, q2s.at[d - 1], q2r.at[d - 1], along(False, d)))
    q3 = [send(qh.at[c, s_me], qh.at[c, s_me], q3s.at[0], q3r.at[0], sibling)]
    outs += [merge(k) for k in range(2, CHUNKS)]
    for d in (1, 2, 3):
        q2[d - 1].wait_recv()
        s = mod4(s_me + 4 - d)
        q3.append(send(qh.at[c, s], qh.at[c, s], q3s.at[d], q3r.at[d], sibling))
    for copy in q3:
        copy.wait_recv()
    sent += q1 + q2 + q3

    for j in range(8):
        parts = []
        for k in (2 * j, 2 * j + 1):
            parts += [qh[0, k % 4, k // 4], qh[1, k // 4, k % 4]]
        term = jnp.dot(
            gbuf[:, j * 768 : (j + 1) * 768], jnp.concatenate(parts, axis=0), preferred_element_type=F32
        )
        if j == 0:
            pacc[...] = term
        else:
            pacc[...] += term

    for k in range(8):
        psend[k, :PIECE] = pacc[k * PIECE : (k + 1) * PIECE]
        psend[k, PIECE:] = sq[...]
    p1 = []
    for e in range(1, 8):
        other = lax.rem(r + e, 8)
        p1.append(send(psend.at[other], precv.at[e - 1], p1s.at[e - 1], p1r.at[e - 1], (f, other)))
    total = psend[r]
    for e in range(1, 8):
        p1[e - 1].wait_recv()
        total = total + precv[e - 1]
    pall[r] = total[:PIECE].astype(BF16)
    p2 = []
    for e in range(1, 8):
        other = lax.rem(r + e, 8)
        p2.append(send(pall.at[r], pall.at[r], p2s.at[e - 1], p2r.at[e - 1], (f, other)))
    for copy in p2:
        copy.wait_recv()
    sent += p1 + p2

    p_full = pall[...].reshape(ROWS, RANK)
    pt[...] = p_full.T
    my_rows = pl.ds(pl.multiple_of(r * 16, 16), 16)
    gsend[0, :16] = jnp.dot(pt[my_rows, :], p_full, preferred_element_type=F32)
    gsend[0, 16:] = total[PIECE:]
    gx = [send(gsend.at[0], gxr.at[d - 1], gxs.at[d - 1], gxq.at[d - 1], on_x(d)) for d in (1, 2, 3)]

    def right(part):
        def pair(j, _):
            cols = [
                gbuf[:, pl.ds(pl.multiple_of(j * 768 + k * 384 + part * 128, 128), 128)] for k in (0, 1)
            ]
            block = jnp.dot(pt[...], jnp.concatenate(cols, axis=1), preferred_element_type=F32).astype(BF16)
            for k in (0, 1):
                for c2 in (0, 1):
                    for z2 in range(4):
                        yl[c2, part, tile_of(part, j // 2, lax.rem(j, 2) * 2 + k, z2)] = block[
                            c2 * 64 + z2 * 16 : c2 * 64 + z2 * 16 + 16, k * 128 : (k + 1) * 128
                        ]
            return 0

        lax.fori_loop(0, 8, pair, 0)
        return send(yl.at[1 - c, part], yr.at[part], cs.at[part], cr.at[part], sibling)

    order = ((z, x, y), (x, y, z), (y, z, x))
    ways = ((on_z, on_x, on_y), (on_x, on_y, on_z), (on_y, on_z, on_x))

    core = [right(0)]
    for copy in gx:
        copy.wait_recv()
    gsend[1] = gsend[0] + gxr[0] + gxr[1] + gxr[2]
    gyc = [send(gsend.at[1], gyr.at[d - 1], gys.at[d - 1], gyq.at[d - 1], on_y(d)) for d in (1, 2, 3)]
    core.append(right(1))
    for copy in gyc:
        copy.wait_recv()
    gsum = gsend[1] + gyr[0] + gyr[1] + gyr[2]
    gmat[r] = gsum[:16]
    ga = []
    for e in range(1, 8):
        other = lax.rem(r + e, 8)
        ga.append(send(gmat.at[r], gmat.at[r], gas.at[e - 1], gaq.at[e - 1], (f, other)))
    core.append(right(2))
    sent += gx + gyc + ga + core

    def add_core(part):
        core[part].wait_recv()

        def some(i, _):
            at = pl.ds(i * 8, 8)
            yc[part, at] = (yl[c, part, at].astype(F32) + yr[part, at].astype(F32)).astype(BF16)
            return 0

        lax.fori_loop(0, 8, some, 0)
        a0 = order[part][0]
        return [
            send(
                yc.at[part, pl.ds(mod4(a0 + d) * 16, 16)],
                rs1.at[part, d - 1],
                r1s.at[part, d - 1],
                r1r.at[part, d - 1],
                ways[part][0](d),
            )
            for d in (1, 2, 3)
        ]

    s1 = [add_core(part) for part in range(3)]

    for copy in ga:
        copy.wait_recv()
    aug[:, :RANK] = gmat[...].reshape(RANK, RANK)
    rows_i = lax.broadcasted_iota(jnp.int32, (RANK, RANK), 0)
    cols_i = lax.broadcasted_iota(jnp.int32, (RANK, RANK), 1)
    aug[:, RANK:] = jnp.where(rows_i == cols_i, 1.0, 0.0).astype(F32)
    sub = lax.broadcasted_iota(jnp.int32, (8, 128), 0)

    def panel(k, _):
        base = pl.multiple_of(k * 8, 8)
        rowp = aug[pl.ds(base, 8), :RANK]
        ext = aug[pl.ds(base, 8), RANK:]
        turned = pltpu.roll(rowp, lax.rem(128 - base, 128), 1)
        col = [jnp.broadcast_to(turned[:, j : j + 1], (8, 128)) for j in range(8)]
        for j in range(8):
            pivot = jnp.broadcast_to(col[j][j : j + 1, :], (8, 128))
            inv = lax.rsqrt(pivot)
            inv = inv * (1.5 - 0.5 * pivot * inv * inv)
            low = jnp.where(sub > j, col[j] * inv, 0.0)
            for m in range(j + 1, 8):
                col[m] = col[m] - low * jnp.broadcast_to(low[m : m + 1, :], (8, 128))
            row_r = jnp.broadcast_to(rowp[j : j + 1, :], (8, 128)) * inv
            row_e = jnp.broadcast_to(ext[j : j + 1, :], (8, 128)) * inv
            rowp = jnp.where(sub == j, row_r, rowp - low * row_r)
            ext = jnp.where(sub == j, row_e, ext - low * row_e)
        wbuf[pl.ds(base, 8), :] = ext
        v1, v2, v3 = split3(rowp)
        e1, e2, e3 = split3(ext)
        left = jnp.concatenate([v1, v1, v2, v2, v1, v3], axis=0).T.astype(BF16)
        top = jnp.concatenate([v1, v2, v1, v2, v3, v1], axis=0)
        more = jnp.concatenate([e1, e2, e1, e2, e3, e1], axis=0)
        both = jnp.concatenate([top, more], axis=1).astype(BF16)
        aug[...] -= jnp.dot(left, both, preferred_element_type=F32)
        return 0

    lax.fori_loop(0, 8, panel, 0)

    def add(part, own, came, out, waits, n):
        for copy in waits[part]:
            copy.wait_recv()
        value = own.astype(F32)
        for d in (0, 1, 2):
            value = value + came[part, d].astype(F32)
        out[part] = value.astype(BF16)

    s2, s3, g1, g2, g3, sib = [], [], [], [], [], []
    for part in range(3):
        a0, a1, _ = order[part]
        add(part, yc[part, pl.ds(a0 * 16, 16)], rs1, t1, s1, 16)
        s2.append([
            send(
                t1.at[part, pl.ds(mod4(a1 + d) * 4, 4)],
                rs2.at[part, d - 1],
                r2s.at[part, d - 1],
                r2r.at[part, d - 1],
                ways[part][1](d),
            )
            for d in (1, 2, 3)
        ])
    for part in range(3):
        _, a1, a2 = order[part]
        add(part, t1[part, pl.ds(a1 * 4, 4)], rs2, t2, s2, 4)
        s3.append([
            send(
                t2.at[part, pl.ds(mod4(a2 + d), 1)],
                rs3.at[part, d - 1],
                r3s.at[part, d - 1],
                r3r.at[part, d - 1],
                ways[part][2](d),
            )
            for d in (1, 2, 3)
        ])
    for part in range(3):
        a0, a1, a2 = order[part]
        for copy in s3[part]:
            copy.wait_recv()
        value = t2[part, pl.ds(a2, 1)].astype(F32)
        for d in (0, 1, 2):
            value = value + rs3[part, d].astype(F32)
        mine = pl.ds(a0 * 16 + a1 * 4 + a2, 1)
        gy[c, part, mine] = value.astype(BF16)
        here = gy.at[c, part, mine]
        g1.append([
            send(here, here, a1s.at[part, d - 1], a1r.at[part, d - 1], ways[part][2](d)) for d in (1, 2, 3)
        ])
    for part in range(3):
        a0, a1, _ = order[part]
        for copy in g1[part]:
            copy.wait_recv()
        here = gy.at[c, part, pl.ds(a0 * 16 + a1 * 4, 4)]
        g2.append([
            send(here, here, a2s.at[part, d - 1], a2r.at[part, d - 1], ways[part][1](d)) for d in (1, 2, 3)
        ])
    for part in range(3):
        a0 = order[part][0]
        for copy in g2[part]:
            copy.wait_recv()
        here = gy.at[c, part, pl.ds(a0 * 16, 16)]
        g3.append([
            send(here, here, a3s.at[part, d - 1], a3r.at[part, d - 1], ways[part][0](d)) for d in (1, 2, 3)
        ])
        sib.append([send(here, here, ss.at[part, 0], sr.at[part, 0], sibling)])

    lax.fori_loop(8, 16, panel, 0)

    w = wbuf[...]
    pb = jnp.zeros((ROWS, RANK), F32)
    p_again = pall[...].reshape(ROWS, RANK)
    for piece in split3(w)[::-1]:
        pb = pb + lax.dot_general(
            p_again, piece.astype(BF16), (((1,), (1,)), ((), ())), preferred_element_type=F32
        )
    basis_ref[...] = pb
    bmat_ref[...] = (
        jnp.dot(pb, w, preferred_element_type=F32, precision=lax.Precision.HIGHEST) * 0.125
    ).astype(BF16)
    squares = jnp.sum(gsum[16:])
    root_mean = jnp.sqrt(jnp.full((1, RANK), squares) / (8 * D * D) + 1e-06)
    scale = jnp.minimum(1.0, clip_ref[0, 0] / root_mean) * 0.125
    w_ref[...] = w * scale

    for d in (1, 2, 3):
        for part in range(3):
            g3[part][d - 1].wait_recv()
            here = gy.at[c, part, pl.ds(mod4(order[part][0] + 4 - d) * 16, 16)]
            sib[part].append(send(here, here, ss.at[part, d], sr.at[part, d], sibling))
    ytc = []
    for part in range(3):
        ytc.append(pltpu.make_async_copy(gy.at[c, part], yt_out.at[c, part], yt_sem.at[0, part]))
        ytc[-1].start()
    for part in range(3):
        for copy in sib[part]:
            copy.wait_recv()
        ytc.append(pltpu.make_async_copy(gy.at[1 - c, part], yt_out.at[1 - c, part], yt_sem.at[1, part]))
        ytc[-1].start()
    for group in (s1, s2, s3, g1, g2, g3, sib):
        for copies in group:
            sent += copies
    for copy in sent:
        copy.wait_send()
    for copy in outs + ytc:
        copy.wait()


def update(merged_ref, yt_ref, bmat_ref, basis_ref, w_ref, new_ref, basis_out, q_out):
    f = lax.axis_index("fsdp")
    j = pl.program_id(0)

    def columns(part, x, y):
        tiles = [yt_ref[c, part, tile_of(part, x, y, z)] for c in (0, 1) for z in range(4)]
        return jnp.concatenate(tiles, axis=0)

    x, y = j // 2, lax.rem(j, 2) * 2
    right = jnp.concatenate([columns(part, x, y + k) for k in (0, 1) for part in range(3)], axis=1)
    for i in range(3):
        rows = slice(i * 128, (i + 1) * 128)
        low = jnp.dot(bmat_ref[rows], right, preferred_element_type=F32)
        new_ref[rows] = (merged_ref[rows].astype(F32) - low).astype(BF16)

    @pl.when(j == 7)
    def _():
        basis_out[...] = basis_ref[...]
        for part in range(3):
            own = columns(part, f // 4, lax.rem(f, 4))
            value = jnp.zeros((RANK, RANK), F32)
            for piece in split3(w_ref[...])[::-1]:
                value = value + jnp.dot(piece.astype(BF16), own, preferred_element_type=F32)
            q_out[part * 128 : (part + 1) * 128] = value.T


def body(grads, errors, q_start, clip_rms):
    dma = pltpu.SemaphoreType.DMA
    vmem = pltpu.VMEM
    hbm = pl.BlockSpec(memory_space=pl.ANY)
    inside = pl.BlockSpec(memory_space=pltpu.VMEM)
    merged, yt, bmat, basis, w = pl.pallas_call(
        exchange,
        out_shape=(
            jax.ShapeDtypeStruct((ROWS, D), BF16),
            jax.ShapeDtypeStruct((2, 3, 64, 16, 128), BF16),
            jax.ShapeDtypeStruct((ROWS, RANK), BF16),
            jax.ShapeDtypeStruct((ROWS, RANK), F32),
            jax.ShapeDtypeStruct((RANK, RANK), F32),
        ),
        in_specs=[pl.BlockSpec(memory_space=pltpu.SMEM), hbm, hbm, inside],
        out_specs=(hbm, hbm, inside, inside, inside),
        scratch_shapes=[
            vmem((ROWS, D), BF16),
            vmem((ROWS, D), BF16),
            vmem((2, 4, 4, HALF, RANK), BF16),
            vmem((ROWS, RANK), F32),
            vmem((8, 128), F32),
            vmem((8, PIECE + 8, RANK), F32),
            vmem((7, PIECE + 8, RANK), F32),
            vmem((8, PIECE, RANK), BF16),
            vmem((RANK, ROWS), BF16),
            vmem((2, 24, RANK), F32),
            vmem((3, 24, RANK), F32),
            vmem((3, 24, RANK), F32),
            vmem((8, 16, RANK), F32),
            vmem((RANK, 2 * RANK), F32),
            vmem((RANK, RANK), F32),
            vmem((2, 3, 64, 16, 128), BF16),
            vmem((3, 64, 16, 128), BF16),
            vmem((3, 64, 16, 128), BF16),
            vmem((3, 3, 16, 16, 128), BF16),
            vmem((3, 3, 4, 16, 128), BF16),
            vmem((3, 3, 1, 16, 128), BF16),
            vmem((3, 16, 16, 128), BF16),
            vmem((3, 4, 16, 128), BF16),
            vmem((2, 3, 64, 16, 128), BF16),
            dma((2, CHUNKS)),
            dma((CHUNKS,)),
            dma((2, 3)),
            dma((3,)),
            dma((3,)),
            dma((3,)),
            dma((3,)),
            dma((4,)),
            dma((4,)),
            dma((7,)),
            dma((7,)),
            dma((7,)),
            dma((7,)),
            dma((3,)),
            dma((3,)),
            dma((3,)),
            dma((3,)),
            dma((7,)),
            dma((7,)),
            dma((3,)),
            dma((3,)),
        ]
        + [dma((3, 3))] * 12
        + [dma((3, 4))] * 2,
        compiler_params=pltpu.CompilerParams(
            collective_id=0, has_side_effects=True, vmem_limit_bytes=48 * 1024 * 1024
        ),
        name="exchange",
    )(clip_rms.reshape(1, 1), grads[0], errors[0], q_start)

    def whole(shape):
        return pl.BlockSpec(shape, lambda j: (0,) * len(shape))

    new_errors, basis, q_out = pl.pallas_call(
        update,
        grid=(8,),
        out_shape=(
            jax.ShapeDtypeStruct((ROWS, D), BF16),
            jax.ShapeDtypeStruct((ROWS, RANK), F32),
            jax.ShapeDtypeStruct((ROWS, RANK), F32),
        ),
        in_specs=[
            pl.BlockSpec((ROWS, 768), lambda j: (0, j)),
            whole((2, 3, 64, 16, 128)),
            whole((ROWS, RANK)),
            whole((ROWS, RANK)),
            whole((RANK, RANK)),
        ],
        out_specs=(
            pl.BlockSpec((ROWS, 768), lambda j: (0, j)),
            whole((ROWS, RANK)),
            whole((ROWS, RANK)),
        ),
        compiler_params=pltpu.CompilerParams(vmem_limit_bytes=48 * 1024 * 1024),
        name="update",
    )(merged, yt, bmat, basis, w)
    return new_errors[None], basis, q_out


def solution(mesh):
    return jax.shard_map(
        body,
        mesh=mesh,
        in_specs=(P("replica", "fsdp", None), P("replica", "fsdp", None), P("fsdp", None), P()),
        out_specs=(P("replica", "fsdp", None), P("fsdp", None), P("fsdp", None)),
        check_vma=False,
    )
```

time: 427 us -> 79.3 us (0.19)
  waiting for transfers between devices: 228 us -> 0 us
  blocking collectives: 126 us -> 0 us
  Pallas kernels: 0 us -> 76.7 us
  other arithmetic: 32.9 us -> 0 us
  matrix products: 23.8 us -> 0 us
  between operations: 15.2 us -> 1.29 us
    psum x2 -> x0, blocking collectives: 126 us -> none  [the longest x1 66.1 us: body(): square_all = lax.psum(squares, ('fsdp', 'replica'))]
    all_gather x2 -> x0, waiting for transfers between devices: 87.5 us -> none  [the longest x1 48 us: body(): lax.all_gather(q_start.astype(jnp.bfloat16), 'fsdp', axis=0, tiled=True)]
    reduce_scatter x1 -> x0, waiting for transfers between devices: 81.8 us -> none  [body(): lax.psum_scatter(lax.dot_general(columns, p_low, (((0,), (0,)), ((), ()))...]
    pallas_call x0 -> x2, Pallas kernels: none -> 76.7 us  [the longest x1 68.5 us: body(): pl.pallas_call(exchange, out_shape=(jax.ShapeDtypeStruct((ROWS, D), BF16)...]
    psum x2 -> x0, waiting for transfers between devices: 58.3 us -> none  [the longest x1 58.3 us: body(): p_sum = lax.psum(p_local, 'replica')]
    another operation x5 -> x0, other arithmetic: 22.9 us -> none  [the longest x3 12.4 us: body(): factor = jnp.linalg.cholesky(gram)]
    dot_general x4 -> x0, matrix products: 22.6 us -> none  [the longest x1 7.91 us: body(): lax.dot_general(p_low, lax.all_gather(q_mean.astype(jnp.bfloat16), 'fsdp'...]
    reduce_sum x1 -> x0, other arithmetic: 6.82 us -> none  [body(): squares = jnp.sum(merged * merged)]
  transfers between devices with their start and end apart: 5 -> 0, of which waited for: 4 -> 0; matrix products, arithmetic and copies ran while one was open for 2% -> 0% of each run, Pallas kernels for 0% -> 0%
where the time goes in v1:
time: 79.3 us; the launch traced here: 79 us
  Pallas kernels  76.7 us (97%)
  between operations  1.29 us (2%)
  local copies, waits for them, and re-layouts  0.92 us (1%)
    pallas_call x1, Pallas kernels, body(): pl.pallas_call(exchange, out_shape=(jax.ShapeDtypeStruct((ROWS, D), BF16)...  68.5 us
    pallas_call x1, Pallas kernels, body(): pl.pallas_call(update, grid=(8,), out_shape=(jax.ShapeDtypeStruct((ROWS,...  8.27 us

profile of v1, /device:TPU:1, one launch (start us, length us, event | category | flops | bytes accessed | tf_op | source)
XLA Modules:
  0.0 79.0 jit_solution(11175260228170155941)
XLA Ops:
  1.3 0.0 copy-start
  1.3 0.9 %copy-done = f32[384,128]{1,0:T(8,128)S(1)} copy-done((f32[384,128]{1,0:T(8,128)S(1)}, f32[384,128]{1,0:T(8,128)}, u32[]{:S(2)}) %copy-start) | copy-done | bytes 196632
  2.2 68.5 %exchange.1 = (bf16[384,6144]{1,0:T(8,128)(2,1)}, bf16[2,3,64,16,128]{4,3,2,1,0:T(8,128)(2,1)S(1)}, bf16[384,128]{1,0:T(8,128)(2,1)S(1)}, f32[384,128]{1,0:T(8,128)S(1)}, f32[128,128]{1,0:T(8,128)S(1)}) custom-call(f32[1,1]{1,0:T(1,128)} %bitcast.4.clip_ref, bf16[384,6144]{1,0:T(8,128)(2,1)} %bitcast.5, bf16[384,6144]{1,0:T(8,128)(2,1)} %bitcast.6, ...), custom_call_target="tpu_custom_call" | custom-call | tf_op jit(solution)/shard_map/exchange/pallas_call | solution.py:475
  70.7 8.3 %update.1 = (bf16[384,6144]{1,0:T(8,128)(2,1)}, f32[384,128]{1,0:T(8,128)}, f32[384,128]{1,0:T(8,128)}) custom-call(bf16[384,6144]{1,0:T(8,128)(2,1)} %get-tuple-element.11.merged_ref, bf16[2,3,64,16,128]{4,3,2,1,0:T(8,128)(2,1)S(1)} %get-tuple-element.12.yt_ref, bf16[384,128]{1,0:T(8,128)(2,1)S(1)} %get-tuple-element.13.bmat_ref, ...), custom_call_target="tpu_custom_call" | custom-call | tf_op jit(solution)/shard_map/update/pallas_call | solution.py:544
Async XLA Ops:
  1.3 0.9 %copy-start = (f32[384,128]{1,0:T(8,128)S(1)}, f32[384,128]{1,0:T(8,128)}, u32[]{:S(2)}) copy-start(f32[384,128]{1,0:T(8,128)} %q_ref.1) | copy-start | bytes 589828

commit v2 on v0

v2 whole, which is shorter than its diff:
```python
import jax
import jax.numpy as jnp
from jax import lax
from jax.experimental import pallas as pl
from jax.experimental.pallas import tpu as pltpu
from jax.sharding import PartitionSpec as P

MESH = pl.DeviceIdType.MESH
F32 = jnp.float32
BF16 = jnp.bfloat16

ROWS = 384
D = 6144
RANK = 128
CHUNKS = 8
CHUNK = ROWS // CHUNKS
HALF = ROWS // 2
PIECE = ROWS // 8
FAR = (2, 1, 3, 0)
OFFSETS = [(dx, dy) for dx in FAR for dy in FAR]


def mod4(v):
    return lax.rem(v + 4, 4)


def split3(v):
    a = v.astype(BF16).astype(F32)
    b = (v - a).astype(BF16).astype(F32)
    return a, b, (v - a - b).astype(BF16).astype(F32)


def exchange(
    clip_ref,
    grads,
    errors,
    q_ref,
    new_ref,
    basis_ref,
    qout_ref,
    gbuf,
    ebuf,
    qin,
    qh,
    pacc,
    sq,
    psend,
    precv,
    pall,
    pt,
    gsend,
    grecv,
    gmat,
    aug,
    wbuf,
    bmat,
    yl,
    yr,
    yc,
    rs,
    gy,
    load_sem,
    qin_sem,
    q1s,
    q1r,
    q2s,
    q2r,
    q3s,
    q3r,
    p1s,
    p1r,
    p2s,
    p2r,
    g1s,
    g1r,
    g2s,
    g2r,
    g3s,
    g3r,
    cs,
    cr,
    rss,
    rsr,
    ags,
    agr,
    fs,
    fr,
):
    f = lax.axis_index("fsdp")
    r = lax.axis_index("replica")
    x, y, z, c = f // 4, lax.rem(f, 4), r // 2, lax.rem(r, 2)
    sibling = (f, z * 2 + 1 - c)

    def at_xy(dx, dy):
        return mod4(x + dx) * 4 + mod4(y + dy)

    def at_z(dz):
        return mod4(z + dz) * 2 + c

    def describe(src, dst, ssem, rsem, device):
        return pltpu.make_async_remote_copy(
            src_ref=src, dst_ref=dst, send_sem=ssem, recv_sem=rsem, device_id=device, device_id_type=MESH
        )

    def send(src, dst, ssem, rsem, device):
        copy = describe(src, dst, ssem, rsem, device)
        copy.start()
        return copy

    sent = []

    qload = pltpu.make_async_copy(q_ref.at[pl.ds(pl.multiple_of(c * HALF, HALF), HALF)], qin, qin_sem)
    qload.start()

    barrier = pltpu.get_barrier_semaphore()
    peers = [sibling]
    for d in (1, 2, 3):
        peers += [(at_xy(d, 0), r), (at_xy(0, d), r), (f, at_z(d)), (f, mod4(z + d) * 2 + 1 - c)]
    for device in peers:
        pl.semaphore_signal(barrier, inc=1, device_id=device, device_id_type=MESH)

    loads = []
    for k in range(CHUNKS):
        rows = pl.ds(k * CHUNK, CHUNK)
        a = pltpu.make_async_copy(grads.at[rows], gbuf.at[rows], load_sem.at[0, k])
        b = pltpu.make_async_copy(errors.at[rows], ebuf.at[rows], load_sem.at[1, k])
        a.start()
        b.start()
        loads.append((a, b))

    s_me, t_me = jnp.where(c == 0, y, x), jnp.where(c == 0, x, y)
    qload.wait()
    qh[c, s_me, t_me] = qin[...].astype(BF16)
    sq[...] = jnp.zeros_like(sq)
    pl.semaphore_wait(barrier, len(peers))

    def along_t(d):
        return (jnp.where(c == 0, at_xy(d, 0), at_xy(0, d)), r)

    def along_s(d):
        return (jnp.where(c == 0, at_xy(0, d), at_xy(d, 0)), r)

    own = qh.at[c, s_me, t_me]
    q1 = [send(own, own, q1s.at[d - 1], q1r.at[d - 1], along_t(d)) for d in (1, 2, 3)]
    q2 = [send(own, own, q2s.at[0, d - 1], q2r.at[d - 1], along_s(d)) for d in (1, 2, 3)]
    q3 = [send(own, own, q3s.at[0], q3r.at[0], sibling)]

    def merge(k):
        a, b = loads[k]
        a.wait()
        b.wait()

        def group(i, _):
            rows = pl.ds(pl.multiple_of(k * CHUNK + i * 16, 16), 16)
            total = jnp.zeros((16, 128), F32)
            for j in range(D // 768):
                cols = pl.ds(j * 768, 768)
                m = gbuf[rows, cols].astype(F32) + ebuf[rows, cols].astype(F32)
                gbuf[rows, cols] = m.astype(BF16)
                m2 = m * m
                for i2 in range(6):
                    total = total + m2[:, i2 * 128 : (i2 + 1) * 128]
            sq[...] += total[:8] + total[8:]
            return 0

        lax.fori_loop(0, CHUNK // 16, group, 0)

    for k in range(3):
        merge(k)
    for d in (1, 3, 2):
        q1[d - 1].wait_recv()
        here = qh.at[c, s_me, mod4(t_me - d)]
        for e in (2, 1, 3):
            q2.append(send(here, here, q2s.at[d, e - 1], q2r.at[e - 1], along_s(e)))
        q3.append(send(here, here, q3s.at[d], q3r.at[d], sibling))
    for k in range(3, CHUNKS):
        merge(k)
    for d in (1, 3, 2):
        here = qh.at[c, mod4(s_me - d)]
        describe(here, here, q2s.at[0, 0], q2r.at[d - 1], sibling).wait_recv()
        q3.append(send(here, here, q3s.at[3 + d], q3r.at[3 + d], sibling))
    for copy in q3:
        copy.wait_recv()
    sent += q1 + q2 + q3

    for j in range(8):
        parts = []
        for k in (2 * j, 2 * j + 1):
            parts += [qh[0, k % 4, k // 4], qh[1, k // 4, k % 4]]
        term = jnp.dot(
            gbuf[:, j * 768 : (j + 1) * 768], jnp.concatenate(parts, axis=0), preferred_element_type=F32
        )
        if j == 0:
            pacc[...] = term
        else:
            pacc[...] += term

    for k in range(8):
        psend[k, :PIECE] = pacc[k * PIECE : (k + 1) * PIECE]
        psend[k, PIECE:] = sq[...]
    p1 = []
    for e in (4, 3, 5, 2, 6, 1, 7):
        other = lax.rem(r + e, 8)
        p1.append(send(psend.at[other], precv.at[r], p1s.at[e - 1], p1r.at[e - 1], (f, other)))
    precv[r] = psend[r]
    for copy in p1:
        copy.wait_recv()
    total = precv[0]
    for k in range(1, 8):
        total = total + precv[k]
    pall[r] = total[:PIECE].astype(BF16)
    p2 = []
    for e in (4, 3, 5, 2, 6, 1, 7):
        other = lax.rem(r + e, 8)
        p2.append(send(pall.at[r], pall.at[r], p2s.at[e - 1], p2r.at[e - 1], (f, other)))
    for copy in p2:
        copy.wait_recv()
    sent += p1 + p2

    p_full = pall[...].reshape(ROWS, RANK)
    pt[...] = p_full.T
    slot = c * 4 + z
    my_rows = pl.ds(pl.multiple_of(slot * 16, 16), 16)
    gsend[:16] = jnp.dot(pt[my_rows, :], p_full, preferred_element_type=F32)
    gsend[16:] = total[PIECE:]
    g1 = [
        send(gsend, grecv.at[k], g1s.at[k], g1r.at[k], (at_xy(dx, dy), r))
        for k, (dx, dy) in enumerate(OFFSETS[:-1])
    ]

    core, rsends = [], []

    def multiply(k):
        g = at_xy(*OFFSETS[k])
        cols = gbuf[:, pl.ds(pl.multiple_of(g * ROWS, 128), ROWS)]
        yl[g] = jnp.dot(pt[...], cols, preferred_element_type=F32).astype(BF16)
        theirs = yl.at[g, pl.ds(pl.multiple_of((1 - c) * 64, 64), 64)]
        core.append(send(theirs, yr.at[g], cs.at[k], cr.at[k], sibling))

    def scatter(k):
        g = at_xy(*OFFSETS[k])
        core[k].wait_recv()
        mine = yl[g, pl.ds(pl.multiple_of(c * 64, 64), 64), :]
        yc[g] = (mine.astype(F32) + yr[g].astype(F32)).astype(BF16)
        here = pl.ds(pl.multiple_of(z * 16, 16), 16)
        for dz in FAR:
            if (dz, k) != (0, 15):
                src = yc.at[g, pl.ds(pl.multiple_of(mod4(z + dz) * 16, 16), 16)]
                rsends.append(send(src, rs.at[f, here], rss.at[k], rsr.at[k], (g, at_z(dz))))
        if k == 15:
            rs[f, here] = yc[f, here, :]

    for k in range(16):
        multiply(k)
        if k >= 2:
            scatter(k - 2)
    scatter(14)
    scatter(15)

    gsum = gsend[...]
    for k in range(15):
        g1[k].wait_recv()
        gsum = gsum + grecv[k]
    gmat[slot] = gsum[:16]
    g2 = [send(gmat.at[slot], gmat.at[slot], g2s.at[d - 1], g2r.at[d - 1], (f, at_z(d))) for d in (1, 2, 3)]

    def came(k, sems, ref):
        dx, dy = OFFSETS[k]
        g = at_xy(-dx, -dy)
        region = ref.at[g, pl.ds(0, 64)] if k < 15 else ref.at[g, pl.ds(0, 48)]
        describe(region, region, sems[0].at[k], sems[1].at[k], sibling).wait_recv()
        return g

    value = jnp.zeros((16, ROWS), F32)
    for k in range(16):
        g = came(k, (rss, rsr), rs)
        for i in range(4):
            value = value + rs[g, i * 16 : (i + 1) * 16, :].astype(F32)
        if k == 8:
            for copy in g2:
                copy.wait_recv()
            side = gmat.at[pl.ds(c * 4, 4)]
            g3 = send(side, side, g3s.at[0], g3r.at[0], sibling)
    mine = pl.ds(pl.multiple_of(c * 64 + z * 16, 16), 16)
    gy[f, mine] = value.astype(BF16)
    asends = []
    for k in range(16):
        g = at_xy(*OFFSETS[k])
        for dz in FAR:
            if (dz, k) != (0, 15):
                here = gy.at[f, mine]
                asends.append(send(here, here, ags.at[k], agr.at[k], (g, at_z(dz))))

    g3.wait_recv()
    aug[:, :RANK] = gmat[...].reshape(RANK, RANK)
    rows_i = lax.broadcasted_iota(jnp.int32, (RANK, RANK), 0)
    cols_i = lax.broadcasted_iota(jnp.int32, (RANK, RANK), 1)
    aug[:, RANK:] = jnp.where(rows_i == cols_i, 1.0, 0.0).astype(F32)
    sub = lax.broadcasted_iota(jnp.int32, (8, 128), 0)

    def panel(k, _):
        base = pl.multiple_of(k * 8, 8)
        rowp = aug[pl.ds(base, 8), :RANK]
        ext = aug[pl.ds(base, 8), RANK:]
        turned = pltpu.roll(rowp, lax.rem(128 - base, 128), 1)
        col = [jnp.broadcast_to(turned[:, j : j + 1], (8, 128)) for j in range(8)]
        for j in range(8):
            pivot = jnp.broadcast_to(col[j][j : j + 1, :], (8, 128))
            inv = lax.rsqrt(pivot)
            inv = inv * (1.5 - 0.5 * pivot * inv * inv)
            low = jnp.where(sub > j, col[j] * inv, 0.0)
            for m in range(j + 1, 8):
                col[m] = col[m] - low * jnp.broadcast_to(low[m : m + 1, :], (8, 128))
            row_r = jnp.broadcast_to(rowp[j : j + 1, :], (8, 128)) * inv
            row_e = jnp.broadcast_to(ext[j : j + 1, :], (8, 128)) * inv
            rowp = jnp.where(sub == j, row_r, rowp - low * row_r)
            ext = jnp.where(sub == j, row_e, ext - low * row_e)
        wbuf[pl.ds(base, 8), :] = ext
        v1, v2, v3 = split3(rowp)
        e1, e2, e3 = split3(ext)
        left = jnp.concatenate([v1, v1, v2, v2, v1, v3], axis=0).T.astype(BF16)
        top = jnp.concatenate([v1, v2, v1, v2, v3, v1], axis=0)
        more = jnp.concatenate([e1, e2, e1, e2, e3, e1], axis=0)
        both = jnp.concatenate([top, more], axis=1).astype(BF16)
        aug[...] -= jnp.dot(left, both, preferred_element_type=F32)
        return 0

    lax.fori_loop(0, 16, panel, 0)

    w = wbuf[...]
    pb = jnp.zeros((ROWS, RANK), F32)
    p_again = pall[...].reshape(ROWS, RANK)
    for piece in split3(w)[::-1]:
        pb = pb + lax.dot_general(
            p_again, piece.astype(BF16), (((1,), (1,)), ((), ())), preferred_element_type=F32
        )
    basis_ref[...] = pb
    bmat[...] = (
        jnp.dot(pb, w, preferred_element_type=F32, precision=lax.Precision.HIGHEST) * 0.125
    ).astype(BF16)

    passed = []

    def forward(k):
        g = came(k, (ags, agr), gy)
        here = gy.at[g, pl.ds(pl.multiple_of(c * 64, 64), 64)]
        passed.append(send(here, here, fs.at[k], fr.at[k], sibling))

    def update(k):
        dx, dy = OFFSETS[k]
        g = at_xy(-dx, -dy)
        passed[k].wait_recv()
        cols = pl.ds(pl.multiple_of(g * ROWS, 128), ROWS)
        low = jnp.dot(bmat[...], gy[g], preferred_element_type=F32)
        new_ref[:, cols] = (gbuf[:, cols].astype(F32) - low).astype(BF16)

    for k in range(16):
        forward(k)
        if k >= 3:
            update(k - 3)
    for k in (13, 14, 15):
        update(k)

    squares = jnp.sum(gsum[16:])
    root_mean = jnp.sqrt(jnp.full((1, RANK), squares) / (8 * D * D) + 1e-06)
    scale = jnp.minimum(1.0, clip_ref[0, 0] / root_mean) * 0.125
    block = gy[f]
    value = jnp.zeros((RANK, ROWS), F32)
    for piece in split3(wbuf[...])[::-1]:
        value = value + jnp.dot(piece.astype(BF16), block, preferred_element_type=F32)
    qout_ref[...] = value.T * scale

    for copy in sent + g1 + g2 + [g3] + core + passed:
        copy.wait_send()
    for sems, ref in ((rss, yc), (ags, gy)):
        for k in range(16):
            region = ref.at[0, pl.ds(0, 64)] if k < 15 else ref.at[0, pl.ds(0, 48)]
            describe(region, region, sems.at[k], rsr.at[k], sibling).wait_send()


def body(grads, errors, q_start, clip_rms):
    dma = pltpu.SemaphoreType.DMA
    vmem = pltpu.VMEM
    hbm = pl.BlockSpec(memory_space=pltpu.HBM)
    inside = pl.BlockSpec(memory_space=pltpu.VMEM)
    new_errors, basis, q_out = pl.pallas_call(
        exchange,
        out_shape=(
            jax.ShapeDtypeStruct((ROWS, D), BF16),
            jax.ShapeDtypeStruct((ROWS, RANK), F32),
            jax.ShapeDtypeStruct((ROWS, RANK), F32),
        ),
        in_specs=[pl.BlockSpec(memory_space=pltpu.SMEM), hbm, hbm, hbm],
        out_specs=(inside, inside, inside),
        scratch_shapes=[
            vmem((ROWS, D), BF16),
            vmem((ROWS, D), BF16),
            vmem((HALF, RANK), F32),
            vmem((2, 4, 4, HALF, RANK), BF16),
            vmem((ROWS, RANK), F32),
            vmem((8, 128), F32),
            vmem((8, PIECE + 8, RANK), F32),
            vmem((8, PIECE + 8, RANK), F32),
            vmem((8, PIECE, RANK), BF16),
            vmem((RANK, ROWS), BF16),
            vmem((24, RANK), F32),
            vmem((15, 24, RANK), F32),
            vmem((8, 16, RANK), F32),
            vmem((RANK, 2 * RANK), F32),
            vmem((RANK, RANK), F32),
            vmem((ROWS, RANK), BF16),
            vmem((16, RANK, ROWS), BF16),
            vmem((16, 64, ROWS), BF16),
            vmem((16, 64, ROWS), BF16),
            vmem((16, 64, ROWS), BF16),
            vmem((16, RANK, ROWS), BF16),
            dma((2, CHUNKS)),
            dma(()),
            dma((3,)),
            dma((3,)),
            dma((4, 3)),
            dma((3,)),
            dma((7,)),
            dma((7,)),
            dma((7,)),
            dma((7,)),
            dma((7,)),
            dma((7,)),
            dma((15,)),
            dma((15,)),
            dma((3,)),
            dma((3,)),
            dma((1,)),
            dma((1,)),
        ]
        + [dma((16,))] * 8,
        compiler_params=pltpu.CompilerParams(
            collective_id=0, has_side_effects=True, vmem_limit_bytes=47 * 1024 * 1024
        ),
        name="exchange",
    )(clip_rms.reshape(1, 1), grads[0], errors[0], q_start)
    return new_errors[None], basis, q_out


def solution(mesh):
    return jax.shard_map(
        body,
        mesh=mesh,
        in_specs=(P("replica", "fsdp", None), P("replica", "fsdp", None), P("fsdp", None), P()),
        out_specs=(P("replica", "fsdp", None), P("fsdp", None), P("fsdp", None)),
        check_vma=False,
    )
```

time: 427 us -> 70.7 us (0.17)
  waiting for transfers between devices: 228 us -> 0 us
  blocking collectives: 126 us -> 0 us
  Pallas kernels: 0 us -> 64.8 us
  other arithmetic: 32.9 us -> 0 us
  matrix products: 23.8 us -> 0 us
  between operations: 15.2 us -> 1.3 us
  local copies, waits for them, and re-layouts: 0.1 us -> 4.46 us
    psum x2 -> x0, blocking collectives: 126 us -> none  [the longest x1 66.1 us: body(): square_all = lax.psum(squares, ('fsdp', 'replica'))]
    all_gather x2 -> x0, waiting for transfers between devices: 87.5 us -> none  [the longest x1 48 us: body(): lax.all_gather(q_start.astype(jnp.bfloat16), 'fsdp', axis=0, tiled=True)]
    reduce_scatter x1 -> x0, waiting for transfers between devices: 81.8 us -> none  [body(): lax.psum_scatter(lax.dot_general(columns, p_low, (((0,), (0,)), ((), ()))...]
    pallas_call x0 -> x1, Pallas kernels: none -> 64.8 us  [body(): pl.pallas_call(exchange, out_shape=(jax.ShapeDtypeStruct((ROWS, D), BF16)...]
    psum x2 -> x0, waiting for transfers between devices: 58.3 us -> none  [the longest x1 58.3 us: body(): p_sum = lax.psum(p_local, 'replica')]
    another operation x5 -> x0, other arithmetic: 22.9 us -> none  [the longest x3 12.4 us: body(): factor = jnp.linalg.cholesky(gram)]
    dot_general x4 -> x0, matrix products: 22.6 us -> none  [the longest x1 7.91 us: body(): lax.dot_general(p_low, lax.all_gather(q_mean.astype(jnp.bfloat16), 'fsdp'...]
    reduce_sum x1 -> x0, other arithmetic: 6.82 us -> none  [body(): squares = jnp.sum(merged * merged)]
  transfers between devices with their start and end apart: 5 -> 0, of which waited for: 4 -> 0; matrix products, arithmetic and copies ran while one was open for 2% -> 0% of each run, Pallas kernels for 0% -> 0%
where the time goes in v2:
time: 70.7 us; the launch traced here: 70.6 us
  Pallas kernels  64.8 us (92%)
  local copies, waits for them, and re-layouts  4.46 us (6%)
  between operations  1.3 us (2%)
    pallas_call x1, Pallas kernels, body(): pl.pallas_call(exchange, out_shape=(jax.ShapeDtypeStruct((ROWS, D), BF16)...  64.8 us
    unnamed x5, local copies, waits for them, and re-layouts  4.46 us

profile of v2, /device:TPU:1, one launch (start us, length us, event | category | flops | bytes accessed | tf_op | source)
XLA Modules:
  0.0 70.6 jit_solution(5291959079967026284)
XLA Ops:
  1.3 0.0 copy-start
  1.3 0.9 %copy-done = f32[384,128]{1,0:T(8,128)S(1)} copy-done((f32[384,128]{1,0:T(8,128)S(1)}, f32[384,128]{1,0:T(8,128)}, u32[]{:S(2)}) %copy-start) | copy-done | bytes 196632
  2.2 64.8 %exchange.1 = (bf16[384,6144]{1,0:T(8,128)(2,1)S(1)}, f32[384,128]{1,0:T(8,128)S(1)}, f32[384,128]{1,0:T(8,128)S(1)}) custom-call(f32[1,1]{1,0:T(1,128)} %bitcast.4.clip_ref, bf16[384,6144]{1,0:T(8,128)(2,1)} %bitcast.6, bf16[384,6144]{1,0:T(8,128)(2,1)} %bitcast.7, f32[384,128]{1,0:T(8,128)S(1)} %copy-done), custom_call_target="tpu_custom_call" | custom-call | tf_op jit(solution)/shard_map/exchange/pallas_call | solution.py:386
  67.0 2.2 %copy.11 = bf16[1,384,6144]{2,1,0:T(8,128)(2,1)} copy(bf16[1,384,6144]{2,1,0:T(8,128)(2,1)S(1)} %bitcast.5) | data formatting | bytes 9437184
  69.2 0.7 copy.12
  69.9 0.7 copy.13
Async XLA Ops:
  1.3 0.9 %copy-start = (f32[384,128]{1,0:T(8,128)S(1)}, f32[384,128]{1,0:T(8,128)}, u32[]{:S(2)}) copy-start(f32[384,128]{1,0:T(8,128)} %q_ref.1) | copy-start | bytes 589828

commit v3 on v2

--- a/solution.py
+++ b/solution.py
@@ -17,7 +17,7 @@
 HALF = ROWS // 2
 PIECE = ROWS // 8
 FAR = (2, 1, 3, 0)
-OFFSETS = [(dx, dy) for dx in FAR for dy in FAR]
+PLANE = [(d, e) for d in FAR for e in FAR][:-1]
 
 
 def mod4(v):
@@ -28,6 +28,10 @@
     a = v.astype(BF16).astype(F32)
     b = (v - a).astype(BF16).astype(F32)
     return a, b, (v - a - b).astype(BF16).astype(F32)
+
+
+def tile_of(part, x, y, z):
+    return (z * 16 + x * 4 + y, x * 16 + y * 4 + z, y * 16 + z * 4 + x)[part]
 
 
 def exchange(
@@ -49,7 +53,8 @@
     pall,
     pt,
     gsend,
-    grecv,
+    gxr,
+    gyr,
     gmat,
     aug,
     wbuf,
@@ -57,7 +62,9 @@
     yl,
     yr,
     yc,
-    rs,
+    rs1,
+    t1,
+    rs2,
     gy,
     load_sem,
     qin_sem,
@@ -71,18 +78,24 @@
     p1r,
     p2s,
     p2r,
-    g1s,
-    g1r,
+    gxs,
+    gxq,
+    gys,
+    gyq,
     g2s,
     g2r,
     g3s,
     g3r,
     cs,
     cr,
-    rss,
-    rsr,
-    ags,
-    agr,
+    r1s,
+    r1r,
+    a2s,
+    a2r,
+    r2s,
+    r2r,
+    a1s,
+    a1r,
     fs,
     fr,
 ):
@@ -196,8 +209,7 @@
             pacc[...] += term
 
     for k in range(8):
-        psend[k, :PIECE] = pacc[k * PIECE : (k + 1) * PIECE]
-        psend[k, PIECE:] = sq[...]
+        psend[k] = pacc[k * PIECE : (k + 1) * PIECE].astype(BF16)
     p1 = []
     for e in (4, 3, 5, 2, 6, 1, 7):
         other = lax.rem(r + e, 8)
@@ -205,10 +217,10 @@
     precv[r] = psend[r]
     for copy in p1:
         copy.wait_recv()
-    total = precv[0]
+    total = precv[0].astype(F32)
     for k in range(1, 8):
-        total = total + precv[k]
-    pall[r] = total[:PIECE].astype(BF16)
+        total = total + precv[k].astype(F32)
+    pall[r] = total.astype(BF16)
     p2 = []
     for e in (4, 3, 5, 2, 6, 1, 7):
         other = lax.rem(r + e, 8)
@@ -221,78 +233,104 @@
     pt[...] = p_full.T
     slot = c * 4 + z
     my_rows = pl.ds(pl.multiple_of(slot * 16, 16), 16)
-    gsend[:16] = jnp.dot(pt[my_rows, :], p_full, preferred_element_type=F32)
-    gsend[16:] = total[PIECE:]
-    g1 = [
-        send(gsend, grecv.at[k], g1s.at[k], g1r.at[k], (at_xy(dx, dy), r))
-        for k, (dx, dy) in enumerate(OFFSETS[:-1])
-    ]
-
-    core, rsends = [], []
-
-    def multiply(k):
-        g = at_xy(*OFFSETS[k])
-        cols = gbuf[:, pl.ds(pl.multiple_of(g * ROWS, 128), ROWS)]
-        yl[g] = jnp.dot(pt[...], cols, preferred_element_type=F32).astype(BF16)
-        theirs = yl.at[g, pl.ds(pl.multiple_of((1 - c) * 64, 64), 64)]
-        core.append(send(theirs, yr.at[g], cs.at[k], cr.at[k], sibling))
-
-    def scatter(k):
-        g = at_xy(*OFFSETS[k])
-        core[k].wait_recv()
-        mine = yl[g, pl.ds(pl.multiple_of(c * 64, 64), 64), :]
-        yc[g] = (mine.astype(F32) + yr[g].astype(F32)).astype(BF16)
-        here = pl.ds(pl.multiple_of(z * 16, 16), 16)
-        for dz in FAR:
-            if (dz, k) != (0, 15):
-                src = yc.at[g, pl.ds(pl.multiple_of(mod4(z + dz) * 16, 16), 16)]
-                rsends.append(send(src, rs.at[f, here], rss.at[k], rsr.at[k], (g, at_z(dz))))
-        if k == 15:
-            rs[f, here] = yc[f, here, :]
-
-    for k in range(16):
-        multiply(k)
-        if k >= 2:
-            scatter(k - 2)
-    scatter(14)
-    scatter(15)
-
-    gsum = gsend[...]
-    for k in range(15):
-        g1[k].wait_recv()
-        gsum = gsum + grecv[k]
-    gmat[slot] = gsum[:16]
+    gsend[0, :16] = jnp.dot(pt[my_rows, :], p_full, preferred_element_type=F32)
+    gsend[0, 16:] = sq[...]
+    gx = [send(gsend.at[0], gxr.at[d - 1], gxs.at[d - 1], gxq.at[d - 1], (at_xy(d, 0), r)) for d in (1, 2, 3)]
+
+    core = []
+    order = ((z, x, y), (x, y, z), (y, z, x))
+
+    def way(part, steps):
+        dx, dy, dz = ((steps[1], steps[2], steps[0]), (steps[0], steps[1], steps[2]), (steps[2], steps[0], steps[1]))[
+            part
+        ]
+        return (at_xy(dx, dy), at_z(dz))
+
+    def multiply(part):
+        for j in range(4):
+            cols = [gbuf[:, pl.ds((4 * j + k) * ROWS + part * 128, 128)] for k in range(4)]
+            block = jnp.dot(pt[...], jnp.concatenate(cols, axis=1), preferred_element_type=F32).astype(BF16)
+            for k in range(4):
+                for c2 in (0, 1):
+                    for z2 in range(4):
+                        at = c2 * 64 + z2 * 16
+                        yl[c2, part, tile_of(part, j, k, z2)] = block[at : at + 16, k * 128 : (k + 1) * 128]
+        core.append(send(yl.at[1 - c, part], yr.at[part], cs.at[part], cr.at[part], sibling))
+
+    def add_core(part):
+        core[part].wait_recv()
+        for k in range(8):
+            at = pl.ds(k * 8, 8)
+            yc[part, at] = (yl[c, part, at].astype(F32) + yr[part, at].astype(F32)).astype(BF16)
+        a0 = order[part][0]
+        return [
+            send(
+                yc.at[part, pl.ds(mod4(a0 + d) * 16, 16)],
+                rs1.at[part, d - 1],
+                r1s.at[part, d - 1],
+                r1r.at[part, d - 1],
+                way(part, (d, 0, 0)),
+            )
+            for d in (2, 1, 3)
+        ]
+
+    def add_line(part):
+        a0, a1, a2 = order[part]
+        for copy in s1[part]:
+            copy.wait_recv()
+        value = yc[part, pl.ds(a0 * 16, 16)].astype(F32)
+        for d in range(3):
+            value = value + rs1[part, d].astype(F32)
+        t1[part] = value.astype(BF16)
+        return [
+            send(
+                t1.at[part, mod4(a1 + d) * 4 + mod4(a2 + e)],
+                rs2.at[part, k],
+                r2s.at[part],
+                r2r.at[part],
+                way(part, (0, d, e)),
+            )
+            for k, (d, e) in enumerate(PLANE)
+        ]
+
+    def add_plane(part):
+        a0, a1, a2 = order[part]
+        describe(rs2.at[part], rs2.at[part], r2s.at[part], r2r.at[part], sibling).wait_recv()
+        value = t1[part, a1 * 4 + a2].astype(F32)
+        for k in range(15):
+            value = value + rs2[part, k].astype(F32)
+        mine = a0 * 16 + a1 * 4 + a2
+        gy[c, part, mine] = value.astype(BF16)
+        here = gy.at[c, part, mine]
+        for d, e in PLANE:
+            send(here, here, a1s.at[part], a1r.at[part], way(part, (0, d, e)))
+
+    multiply(0)
+    multiply(1)
+    s1 = [add_core(0)]
+    multiply(2)
+    s1 += [add_core(1), add_core(2)]
+    for copy in gx:
+        copy.wait_recv()
+    gsend[1] = gsend[0] + gxr[0] + gxr[1] + gxr[2]
+    gy1 = [send(gsend.at[1], gyr.at[d - 1], gys.at[d - 1], gyq.at[d - 1], (at_xy(0, d), r)) for d in (1, 2, 3)]
+    add_line(0)
+    for copy in gy1:
+        copy.wait_recv()
+    gmat[slot] = gsend[1] + gyr[0] + gyr[1] + gyr[2]
     g2 = [send(gmat.at[slot], gmat.at[slot], g2s.at[d - 1], g2r.at[d - 1], (f, at_z(d))) for d in (1, 2, 3)]
-
-    def came(k, sems, ref):
-        dx, dy = OFFSETS[k]
-        g = at_xy(-dx, -dy)
-        region = ref.at[g, pl.ds(0, 64)] if k < 15 else ref.at[g, pl.ds(0, 48)]
-        describe(region, region, sems[0].at[k], sems[1].at[k], sibling).wait_recv()
-        return g
-
-    value = jnp.zeros((16, ROWS), F32)
-    for k in range(16):
-        g = came(k, (rss, rsr), rs)
-        for i in range(4):
-            value = value + rs[g, i * 16 : (i + 1) * 16, :].astype(F32)
-        if k == 8:
-            for copy in g2:
-                copy.wait_recv()
-            side = gmat.at[pl.ds(c * 4, 4)]
-            g3 = send(side, side, g3s.at[0], g3r.at[0], sibling)
-    mine = pl.ds(pl.multiple_of(c * 64 + z * 16, 16), 16)
-    gy[f, mine] = value.astype(BF16)
-    asends = []
-    for k in range(16):
-        g = at_xy(*OFFSETS[k])
-        for dz in FAR:
-            if (dz, k) != (0, 15):
-                here = gy.at[f, mine]
-                asends.append(send(here, here, ags.at[k], agr.at[k], (g, at_z(dz))))
+    add_line(1)
+    add_line(2)
+    for copy in g2:
+        copy.wait_recv()
+    side = gmat.at[pl.ds(c * 4, 4)]
+    g3 = send(side, side, g3s.at[0], g3r.at[0], sibling)
+    for part in range(3):
+        add_plane(part)
 
     g3.wait_recv()
-    aug[:, :RANK] = gmat[...].reshape(RANK, RANK)
+    for k in range(8):
+        aug[k * 16 : (k + 1) * 16, :RANK] = gmat[k, :16]
     rows_i = lax.broadcasted_iota(jnp.int32, (RANK, RANK), 0)
     cols_i = lax.broadcasted_iota(jnp.int32, (RANK, RANK), 1)
     aug[:, RANK:] = jnp.where(rows_i == cols_i, 1.0, 0.0).astype(F32)
@@ -325,7 +363,22 @@
         aug[...] -= jnp.dot(left, both, preferred_element_type=F32)
         return 0
 
-    lax.fori_loop(0, 16, panel, 0)
+    lines, passed = [], []
+
+    def spread(part):
+        a0 = order[part][0]
+        here = gy.at[c, part, pl.ds(a0 * 16, 16)]
+        region = rs2.at[part]
+        describe(region, region, a1s.at[part], a1r.at[part], sibling).wait_recv()
+        lines.append([
+            send(here, here, a2s.at[part, d - 1], a2r.at[part, d - 1], way(part, (d, 0, 0))) for d in (1, 2, 3)
+        ])
+        passed.append([send(here, here, fs.at[part, 0], fr.at[part, 0], sibling)])
+
+    lax.fori_loop(0, 9, panel, 0)
+    for part in range(3):
+        spread(part)
+    lax.fori_loop(9, 16, panel, 0)
 
     w = wbuf[...]
     pb = jnp.zeros((ROWS, RANK), F32)
@@ -339,43 +392,70 @@
         jnp.dot(pb, w, preferred_element_type=F32, precision=lax.Precision.HIGHEST) * 0.125
     ).astype(BF16)
 
-    passed = []
-
-    def forward(k):
-        g = came(k, (ags, agr), gy)
-        here = gy.at[g, pl.ds(pl.multiple_of(c * 64, 64), 64)]
-        passed.append(send(here, here, fs.at[k], fr.at[k], sibling))
-
-    def update(k):
-        dx, dy = OFFSETS[k]
-        g = at_xy(-dx, -dy)
-        passed[k].wait_recv()
-        cols = pl.ds(pl.multiple_of(g * ROWS, 128), ROWS)
-        low = jnp.dot(bmat[...], gy[g], preferred_element_type=F32)
-        new_ref[:, cols] = (gbuf[:, cols].astype(F32) - low).astype(BF16)
-
-    for k in range(16):
-        forward(k)
-        if k >= 3:
-            update(k - 3)
-    for k in (13, 14, 15):
-        update(k)
-
-    squares = jnp.sum(gsum[16:])
+    def right(part, x2, y2):
+        tiles = [gy[c2, part, tile_of(part, x2, y2, z2)] for c2 in (0, 1) for z2 in range(4)]
+        return jnp.concatenate(tiles, axis=0)
+
+    def update(part, places):
+        low = jnp.dot(
+            bmat[...],
+            jnp.concatenate([right(part, x2, y2) for x2, y2 in places], axis=1),
+            preferred_element_type=F32,
+        )
+        for k, (x2, y2) in enumerate(places):
+            cols = pl.ds(pl.multiple_of((x2 * 4 + y2) * ROWS + part * 128, 128), 128)
+            new_ref[:, cols] = (gbuf[:, cols].astype(F32) - low[:, k * 128 : (k + 1) * 128]).astype(BF16)
+
+    def group(part, a0):
+        passed[part][-1].wait_recv()
+        if part == 1:
+            update(part, [(a0, k) for k in range(4)])
+        if part == 2:
+            update(part, [(k, a0) for k in range(4)])
+
+    for part in range(3):
+        group(part, order[part][0])
+    for d in (1, 3, 2):
+        for part in range(3):
+            lines[part][d - 1].wait_recv()
+            here = gy.at[c, part, pl.ds(mod4(order[part][0] - d) * 16, 16)]
+            passed[part].append(send(here, here, fs.at[part, d], fr.at[part, d], sibling))
+        for part in range(3):
+            group(part, mod4(order[part][0] - d))
+    for j in range(4):
+        update(0, [(j, k) for k in range(4)])
+
+    squares = jnp.sum(jnp.sum(gmat[:, 16:], axis=0))
     root_mean = jnp.sqrt(jnp.full((1, RANK), squares) / (8 * D * D) + 1e-06)
     scale = jnp.minimum(1.0, clip_ref[0, 0] / root_mean) * 0.125
-    block = gy[f]
+    block = jnp.concatenate([right(part, x, y) for part in range(3)], axis=1)
     value = jnp.zeros((RANK, ROWS), F32)
     for piece in split3(wbuf[...])[::-1]:
         value = value + jnp.dot(piece.astype(BF16), block, preferred_element_type=F32)
     qout_ref[...] = value.T * scale
 
-    for copy in sent + g1 + g2 + [g3] + core + passed:
+    for group_of in s1 + lines + passed:
+        sent += group_of
+    for copy in sent + gx + gy1 + g2 + [g3] + core:
         copy.wait_send()
-    for sems, ref in ((rss, yc), (ags, gy)):
-        for k in range(16):
-            region = ref.at[0, pl.ds(0, 64)] if k < 15 else ref.at[0, pl.ds(0, 48)]
-            describe(region, region, sems.at[k], rsr.at[k], sibling).wait_send()
+    for part in range(3):
+        region = rs2.at[part]
+        for sems in (r2s, a1s):
+            describe(region, region, sems.at[part], r2r.at[part], sibling).wait_send()
+
+
+def hand_over(new_ref, basis_ref, q_ref, new_out, basis_out, q_out, sems):
+    copies = [
+        pltpu.make_async_copy(basis_ref, basis_out, sems.at[CHUNKS]),
+        pltpu.make_async_copy(q_ref, q_out, sems.at[CHUNKS + 1]),
+    ]
+    for k in range(CHUNKS):
+        rows = pl.ds(k * CHUNK, CHUNK)
+        copies.append(pltpu.make_async_copy(new_ref.at[rows], new_out.at[rows], sems.at[k]))
+    for copy in copies:
+        copy.start()
+    for copy in copies:
+        copy.wait()
 
 
 def body(grads, errors, q_start, clip_rms):
@@ -399,21 +479,24 @@
             vmem((2, 4, 4, HALF, RANK), BF16),
             vmem((ROWS, RANK), F32),
             vmem((8, 128), F32),
-            vmem((8, PIECE + 8, RANK), F32),
-            vmem((8, PIECE + 8, RANK), F32),
+            vmem((8, PIECE, RANK), BF16),
+            vmem((8, PIECE, RANK), BF16),
             vmem((8, PIECE, RANK), BF16),
             vmem((RANK, ROWS), BF16),
-            vmem((24, RANK), F32),
-            vmem((15, 24, RANK), F32),
-            vmem((8, 16, RANK), F32),
+            vmem((2, 24, RANK), F32),
+            vmem((3, 24, RANK), F32),
+            vmem((3, 24, RANK), F32),
+            vmem((8, 24, RANK), F32),
             vmem((RANK, 2 * RANK), F32),
             vmem((RANK, RANK), F32),
             vmem((ROWS, RANK), BF16),
-            vmem((16, RANK, ROWS), BF16),
-            vmem((16, 64, ROWS), BF16),
-            vmem((16, 64, ROWS), BF16),
-            vmem((16, 64, ROWS), BF16),
-            vmem((16, RANK, ROWS), BF16),
+            vmem((2, 3, 64, 16, 128), BF16),
+            vmem((3, 64, 16, 128), BF16),
+            vmem((3, 64, 16, 128), BF16),
+            vmem((3, 3, 16, 16, 128), BF16),
+            vmem((3, 16, 16, 128), BF16),
+            vmem((3, 15, 16, 128), BF16),
+            vmem((2, 3, 64, 16, 128), BF16),
             dma((2, CHUNKS)),
             dma(()),
             dma((3,)),
@@ -426,19 +509,46 @@
             dma((7,)),
             dma((7,)),
             dma((7,)),
-            dma((15,)),
-            dma((15,)),
+            dma((3,)),
+            dma((3,)),
+            dma((3,)),
+            dma((3,)),
             dma((3,)),
             dma((3,)),
             dma((1,)),
             dma((1,)),
-        ]
-        + [dma((16,))] * 8,
+            dma((3,)),
+            dma((3,)),
+            dma((3, 3)),
+            dma((3, 3)),
+            dma((3, 3)),
+            dma((3, 3)),
+            dma((3,)),
+            dma((3,)),
+            dma((3,)),
+            dma((3,)),
+            dma((3, 4)),
+            dma((3, 4)),
+        ],
         compiler_params=pltpu.CompilerParams(
             collective_id=0, has_side_effects=True, vmem_limit_bytes=47 * 1024 * 1024
         ),
         name="exchange",
     )(clip_rms.reshape(1, 1), grads[0], errors[0], q_start)
+    anywhere = pl.BlockSpec(memory_space=pl.ANY)
+    new_errors, basis, q_out = pl.pallas_call(
+        hand_over,
+        out_shape=(
+            jax.ShapeDtypeStruct((ROWS, D), BF16),
+            jax.ShapeDtypeStruct((ROWS, RANK), F32),
+            jax.ShapeDtypeStruct((ROWS, RANK), F32),
+        ),
+        in_specs=[anywhere] * 3,
+        out_specs=(anywhere,) * 3,
+        scratch_shapes=[dma((CHUNKS + 2,))],
+        compiler_params=pltpu.CompilerParams(vmem_limit_bytes=1024 * 1024),
+        name="hand_over",
+    )(new_errors, basis, q_out)
     return new_errors[None], basis, q_out
 
 

time: 70.7 us -> 65.1 us (0.921)
  local copies, waits for them, and re-layouts: 4.46 us -> 0.92 us
  Pallas kernels: 64.8 us -> 62.8 us
    pallas_call x1, Pallas kernels: 64.8 us -> 60.4 us  [body(): pl.pallas_call(exchange, out_shape=(jax.ShapeDtypeStruct((ROWS, D), BF16)...]
    unnamed x5 -> x2, local copies, waits for them, and re-layouts: 4.46 us -> 0.92 us
    pallas_call x0 -> x1, Pallas kernels: none -> 2.39 us  [body(): pl.pallas_call(hand_over, out_shape=(jax.ShapeDtypeStruct((ROWS, D), BF16...]
where the time goes in v3:
time: 65.1 us; the launch traced here: 65 us
  Pallas kernels  62.8 us (96%)
  between operations  1.29 us (2%)
  local copies, waits for them, and re-layouts  0.92 us (1%)
    pallas_call x1, Pallas kernels, body(): pl.pallas_call(exchange, out_shape=(jax.ShapeDtypeStruct((ROWS, D), BF16)...  60.4 us
    pallas_call x1, Pallas kernels, body(): pl.pallas_call(hand_over, out_shape=(jax.ShapeDtypeStruct((ROWS, D), BF16...  2.39 us

profile of v3, /device:TPU:1, one launch (start us, length us, event | category | flops | bytes accessed | tf_op | source)
XLA Modules:
  0.0 65.0 jit_solution(11308009095195027464)
XLA Ops:
  1.3 0.0 copy-start
  1.3 0.9 %copy-done = f32[384,128]{1,0:T(8,128)S(1)} copy-done((f32[384,128]{1,0:T(8,128)S(1)}, f32[384,128]{1,0:T(8,128)}, u32[]{:S(2)}) %copy-start) | copy-done | bytes 196632
  2.2 60.4 %exchange.1 = (bf16[384,6144]{1,0:T(8,128)(2,1)S(1)}, f32[384,128]{1,0:T(8,128)S(1)}, f32[384,128]{1,0:T(8,128)S(1)}) custom-call(f32[1,1]{1,0:T(1,128)} %bitcast.4.clip_ref, bf16[384,6144]{1,0:T(8,128)(2,1)} %bitcast.5, bf16[384,6144]{1,0:T(8,128)(2,1)} %bitcast.6, f32[384,128]{1,0:T(8,128)S(1)} %copy-done), custom_call_target="tpu_custom_call" | custom-call | tf_op jit(solution)/shard_map/exchange/pallas_call | solution.py:466
  62.6 2.4 %hand_over.1 = (bf16[384,6144]{1,0:T(8,128)(2,1)}, f32[384,128]{1,0:T(8,128)}, f32[384,128]{1,0:T(8,128)}) custom-call(bf16[384,6144]{1,0:T(8,128)(2,1)S(1)} %get-tuple-element.9.new_ref, f32[384,128]{1,0:T(8,128)S(1)} %get-tuple-element.10.basis_ref, f32[384,128]{1,0:T(8,128)S(1)} %get-tuple-element.11.q_ref), custom_call_target="tpu_custom_call" | custom-call | tf_op jit(solution)/shard_map/hand_over/pallas_call | solution.py:539
Async XLA Ops:
  1.3 0.9 %copy-start = (f32[384,128]{1,0:T(8,128)S(1)}, f32[384,128]{1,0:T(8,128)}, u32[]{:S(2)}) copy-start(f32[384,128]{1,0:T(8,128)} %q_ref.1) | copy-start | bytes 589828

commit v4 on v3

--- a/solution.py
+++ b/solution.py
@@ -143,7 +143,12 @@
 
     s_me, t_me = jnp.where(c == 0, y, x), jnp.where(c == 0, x, y)
     qload.wait()
-    qh[c, s_me, t_me] = qin[...].astype(BF16)
+    filled = pl.ds(pl.multiple_of(c * 64, 64), HALF)
+    for s in range(4):
+        for t in range(4):
+            qh[0, s, t, HALF:] = jnp.zeros((64, RANK), BF16)
+            qh[1, s, t, :64] = jnp.zeros((64, RANK), BF16)
+    qh[c, s_me, t_me, filled] = qin[...].astype(BF16)
     sq[...] = jnp.zeros_like(sq)
     pl.semaphore_wait(barrier, len(peers))
 
@@ -153,7 +158,7 @@
     def along_s(d):
         return (jnp.where(c == 0, at_xy(0, d), at_xy(d, 0)), r)
 
-    own = qh.at[c, s_me, t_me]
+    own = qh.at[c, s_me, t_me, filled]
     q1 = [send(own, own, q1s.at[d - 1], q1r.at[d - 1], along_t(d)) for d in (1, 2, 3)]
     q2 = [send(own, own, q2s.at[0, d - 1], q2r.at[d - 1], along_s(d)) for d in (1, 2, 3)]
     q3 = [send(own, own, q3s.at[0], q3r.at[0], sibling)]
@@ -182,31 +187,45 @@
         merge(k)
     for d in (1, 3, 2):
         q1[d - 1].wait_recv()
-        here = qh.at[c, s_me, mod4(t_me - d)]
+        here = qh.at[c, s_me, mod4(t_me - d), filled]
         for e in (2, 1, 3):
             q2.append(send(here, here, q2s.at[d, e - 1], q2r.at[e - 1], along_s(e)))
         q3.append(send(here, here, q3s.at[d], q3r.at[d], sibling))
     for k in range(3, CHUNKS):
         merge(k)
-    for d in (1, 3, 2):
-        here = qh.at[c, mod4(s_me - d)]
-        describe(here, here, q2s.at[0, 0], q2r.at[d - 1], sibling).wait_recv()
-        q3.append(send(here, here, q3s.at[3 + d], q3r.at[3 + d], sibling))
-    for copy in q3:
-        copy.wait_recv()
-    sent += q1 + q2 + q3
-
-    for j in range(8):
-        parts = []
-        for k in (2 * j, 2 * j + 1):
-            parts += [qh[0, k % 4, k // 4], qh[1, k // 4, k % 4]]
+    def add_p(half, s, first=False):
+        cols = []
+        for t in range(4):
+            g = jnp.where(half == 0, t * 4 + s, s * 4 + t)
+            cols.append(gbuf[:, pl.ds(pl.multiple_of(g * ROWS + half * 128, 128), 256)])
         term = jnp.dot(
-            gbuf[:, j * 768 : (j + 1) * 768], jnp.concatenate(parts, axis=0), preferred_element_type=F32
+            jnp.concatenate(cols, axis=1), qh[half, s].reshape(1024, RANK), preferred_element_type=F32
         )
-        if j == 0:
+        if first:
             pacc[...] = term
         else:
             pacc[...] += term
+
+    def pass_q(d):
+        here = qh.at[c, mod4(s_me - d), :, filled]
+        describe(here, here, q2s.at[0, 0], q2r.at[d - 1], sibling).wait_recv()
+        q3.append(send(here, here, q3s.at[3 + d], q3r.at[3 + d], sibling))
+        add_p(c, mod4(s_me - d))
+
+    add_p(c, s_me, True)
+    pass_q(1)
+    for copy in q3[:4]:
+        copy.wait_recv()
+    add_p(1 - c, t_me)
+    pass_q(3)
+    q3[4].wait_recv()
+    add_p(1 - c, mod4(t_me - 1))
+    pass_q(2)
+    q3[5].wait_recv()
+    add_p(1 - c, mod4(t_me - 3))
+    q3[6].wait_recv()
+    add_p(1 - c, mod4(t_me - 2))
+    sent += q1 + q2 + q3
 
     for k in range(8):
         psend[k] = pacc[k * PIECE : (k + 1) * PIECE].astype(BF16)
@@ -231,11 +250,6 @@
 
     p_full = pall[...].reshape(ROWS, RANK)
     pt[...] = p_full.T
-    slot = c * 4 + z
-    my_rows = pl.ds(pl.multiple_of(slot * 16, 16), 16)
-    gsend[0, :16] = jnp.dot(pt[my_rows, :], p_full, preferred_element_type=F32)
-    gsend[0, 16:] = sq[...]
-    gx = [send(gsend.at[0], gxr.at[d - 1], gxs.at[d - 1], gxq.at[d - 1], (at_xy(d, 0), r)) for d in (1, 2, 3)]
 
     core = []
     order = ((z, x, y), (x, y, z), (y, z, x))
@@ -307,6 +321,13 @@
 
     multiply(0)
     multiply(1)
+
+    slot = c * 4 + z
+    my_rows = pl.ds(pl.multiple_of(slot * 16, 16), 16)
+    gsend[0, :16] = jnp.dot(pt[my_rows, :], p_full, preferred_element_type=F32)
+    gsend[0, 16:] = sq[...]
+    gx = [send(gsend.at[0], gxr.at[d - 1], gxs.at[d - 1], gxq.at[d - 1], (at_xy(d, 0), r)) for d in (1, 2, 3)]
+
     s1 = [add_core(0)]
     multiply(2)
     s1 += [add_core(1), add_core(2)]
@@ -378,6 +399,14 @@
     lax.fori_loop(0, 9, panel, 0)
     for part in range(3):
         spread(part)
+    for group_of in s1:
+        sent += group_of
+    for copy in sent + gx + gy1 + g2 + [g3] + core:
+        copy.wait_send()
+    for part in range(3):
+        region = rs2.at[part]
+        for sems in (r2s, a1s):
+            describe(region, region, sems.at[part], r2r.at[part], sibling).wait_send()
     lax.fori_loop(9, 16, panel, 0)
 
     w = wbuf[...]
@@ -406,22 +435,28 @@
             cols = pl.ds(pl.multiple_of((x2 * 4 + y2) * ROWS + part * 128, 128), 128)
             new_ref[:, cols] = (gbuf[:, cols].astype(F32) - low[:, k * 128 : (k + 1) * 128]).astype(BF16)
 
-    def group(part, a0):
-        passed[part][-1].wait_recv()
-        if part == 1:
-            update(part, [(a0, k) for k in range(4)])
-        if part == 2:
-            update(part, [(k, a0) for k in range(4)])
-
-    for part in range(3):
-        group(part, order[part][0])
-    for d in (1, 3, 2):
+    def pass_line(d):
         for part in range(3):
             lines[part][d - 1].wait_recv()
             here = gy.at[c, part, pl.ds(mod4(order[part][0] - d) * 16, 16)]
             passed[part].append(send(here, here, fs.at[part, d], fr.at[part, d], sibling))
+
+    def groups(d):
         for part in range(3):
-            group(part, mod4(order[part][0] - d))
+            passed[part][(0, 1, 3, 2)[d]].wait_recv()
+            a0 = mod4(order[part][0] - d)
+            if part == 1:
+                update(part, [(a0, k) for k in range(4)])
+            if part == 2:
+                update(part, [(k, a0) for k in range(4)])
+
+    groups(0)
+    pass_line(1)
+    pass_line(3)
+    groups(1)
+    pass_line(2)
+    groups(3)
+    groups(2)
     for j in range(4):
         update(0, [(j, k) for k in range(4)])
 
@@ -434,14 +469,9 @@
         value = value + jnp.dot(piece.astype(BF16), block, preferred_element_type=F32)
     qout_ref[...] = value.T * scale
 
-    for group_of in s1 + lines + passed:
-        sent += group_of
-    for copy in sent + gx + gy1 + g2 + [g3] + core:
-        copy.wait_send()
-    for part in range(3):
-        region = rs2.at[part]
-        for sems in (r2s, a1s):
-            describe(region, region, sems.at[part], r2r.at[part], sibling).wait_send()
+    for group_of in lines + passed:
+        for copy in group_of:
+            copy.wait_send()
 
 
 def hand_over(new_ref, basis_ref, q_ref, new_out, basis_out, q_out, sems):
@@ -476,7 +506,7 @@
             vmem((ROWS, D), BF16),
             vmem((ROWS, D), BF16),
             vmem((HALF, RANK), F32),
-            vmem((2, 4, 4, HALF, RANK), BF16),
+            vmem((2, 4, 4, 256, RANK), BF16),
             vmem((ROWS, RANK), F32),
             vmem((8, 128), F32),
             vmem((8, PIECE, RANK), BF16),

time: 65.1 us -> 62.7 us (0.963)
  Pallas kernels: 62.8 us -> 60.3 us
    pallas_call x1, Pallas kernels: 60.4 us -> 57.9 us  [body(): pl.pallas_call(exchange, out_shape=(jax.ShapeDtypeStruct((ROWS, D), BF16)...]
where the time goes in v4:
time: 62.7 us; the launch traced here: 62.5 us
  Pallas kernels  60.3 us (96%)
  between operations  1.29 us (2%)
  local copies, waits for them, and re-layouts  0.92 us (1%)
    pallas_call x1, Pallas kernels, body(): pl.pallas_call(exchange, out_shape=(jax.ShapeDtypeStruct((ROWS, D), BF16)...  57.9 us
    pallas_call x1, Pallas kernels, body(): pl.pallas_call(hand_over, out_shape=(jax.ShapeDtypeStruct((ROWS, D), BF16...  2.39 us

profile of v4, /device:TPU:1, one launch (start us, length us, event | category | flops | bytes accessed | tf_op | source)
XLA Modules:
  0.0 62.5 jit_solution(7556562441553482535)
XLA Ops:
  1.3 0.0 copy-start
  1.3 0.9 %copy-done = f32[384,128]{1,0:T(8,128)S(1)} copy-done((f32[384,128]{1,0:T(8,128)S(1)}, f32[384,128]{1,0:T(8,128)}, u32[]{:S(2)}) %copy-start) | copy-done | bytes 196632
  2.2 57.9 %exchange.1 = (bf16[384,6144]{1,0:T(8,128)(2,1)S(1)}, f32[384,128]{1,0:T(8,128)S(1)}, f32[384,128]{1,0:T(8,128)S(1)}) custom-call(f32[1,1]{1,0:T(1,128)} %bitcast.4.clip_ref, bf16[384,6144]{1,0:T(8,128)(2,1)} %bitcast.5, bf16[384,6144]{1,0:T(8,128)(2,1)} %bitcast.6, f32[384,128]{1,0:T(8,128)S(1)} %copy-done), custom_call_target="tpu_custom_call" | custom-call | tf_op jit(solution)/shard_map/exchange/pallas_call | solution.py:496
  60.1 2.4 %hand_over.1 = (bf16[384,6144]{1,0:T(8,128)(2,1)}, f32[384,128]{1,0:T(8,128)}, f32[384,128]{1,0:T(8,128)}) custom-call(bf16[384,6144]{1,0:T(8,128)(2,1)S(1)} %get-tuple-element.9.new_ref, f32[384,128]{1,0:T(8,128)S(1)} %get-tuple-element.10.basis_ref, f32[384,128]{1,0:T(8,128)S(1)} %get-tuple-element.11.q_ref), custom_call_target="tpu_custom_call" | custom-call | tf_op jit(solution)/shard_map/hand_over/pallas_call | solution.py:569
Async XLA Ops:
  1.3 0.9 %copy-start = (f32[384,128]{1,0:T(8,128)S(1)}, f32[384,128]{1,0:T(8,128)}, u32[]{:S(2)}) copy-start(f32[384,128]{1,0:T(8,128)} %q_ref.1) | copy-start | bytes 589828

commit v5 on v4

--- a/solution.py
+++ b/solution.py
@@ -251,7 +251,15 @@
     p_full = pall[...].reshape(ROWS, RANK)
     pt[...] = p_full.T
 
-    core = []
+    slot = c * 4 + z
+    my_rows = pl.ds(pl.multiple_of(slot * 16, 16), 16)
+    gsend[0, :16] = jnp.dot(pt[my_rows, :], p_full, preferred_element_type=F32)
+    gsend[0, 16:] = sq[...]
+    gx = [
+        send(gsend.at[0], gxr.at[k], gxs.at[k], gxq.at[k], (at_xy(dx, dy), r)) for k, (dx, dy) in enumerate(PLANE)
+    ]
+
+    core, s1 = {}, ([], [], [])
     order = ((z, x, y), (x, y, z), (y, z, x))
 
     def way(part, steps):
@@ -260,33 +268,38 @@
         ]
         return (at_xy(dx, dy), at_z(dz))
 
-    def multiply(part):
-        for j in range(4):
-            cols = [gbuf[:, pl.ds((4 * j + k) * ROWS + part * 128, 128)] for k in range(4)]
-            block = jnp.dot(pt[...], jnp.concatenate(cols, axis=1), preferred_element_type=F32).astype(BF16)
-            for k in range(4):
-                for c2 in (0, 1):
-                    for z2 in range(4):
-                        at = c2 * 64 + z2 * 16
-                        yl[c2, part, tile_of(part, j, k, z2)] = block[at : at + 16, k * 128 : (k + 1) * 128]
-        core.append(send(yl.at[1 - c, part], yr.at[part], cs.at[part], cr.at[part], sibling))
-
-    def add_core(part):
-        core[part].wait_recv()
-        for k in range(8):
-            at = pl.ds(k * 8, 8)
-            yc[part, at] = (yl[c, part, at].astype(F32) + yr[part, at].astype(F32)).astype(BF16)
-        a0 = order[part][0]
-        return [
-            send(
-                yc.at[part, pl.ds(mod4(a0 + d) * 16, 16)],
-                rs1.at[part, d - 1],
-                r1s.at[part, d - 1],
-                r1r.at[part, d - 1],
-                way(part, (d, 0, 0)),
+    def multiply(part, places):
+        cols = [
+            gbuf[:, pl.ds(pl.multiple_of((x2 * 4 + y2) * ROWS + part * 128, 128), 128)] for x2, y2 in places
+        ]
+        block = jnp.dot(pt[...], jnp.concatenate(cols, axis=1), preferred_element_type=F32).astype(BF16)
+        for k, (x2, y2) in enumerate(places):
+            for c2 in (0, 1):
+                for z2 in range(4):
+                    at = c2 * 64 + z2 * 16
+                    yl[c2, part, tile_of(part, x2, y2, z2)] = block[at : at + 16, k * 128 : (k + 1) * 128]
+
+    def line(part, d):
+        return pl.ds(pl.multiple_of(mod4(order[part][0] + d) * 16, 16), 16)
+
+    def swap(part, d):
+        at = line(part, d)
+        core[part, d] = send(yl.at[1 - c, part, at], yr.at[part, at], cs.at[part, d], cr.at[part, d], sibling)
+
+    def add_core(part, d):
+        at = line(part, d)
+        core[part, d].wait_recv()
+        yc[part, at] = (yl[c, part, at].astype(F32) + yr[part, at].astype(F32)).astype(BF16)
+        if d:
+            s1[part].append(
+                send(
+                    yc.at[part, at],
+                    rs1.at[part, d - 1],
+                    r1s.at[part, d - 1],
+                    r1r.at[part, d - 1],
+                    way(part, (d, 0, 0)),
+                )
             )
-            for d in (2, 1, 3)
-        ]
 
     def add_line(part):
         a0, a1, a2 = order[part]
@@ -319,26 +332,28 @@
         for d, e in PLANE:
             send(here, here, a1s.at[part], a1r.at[part], way(part, (0, d, e)))
 
-    multiply(0)
-    multiply(1)
-
-    slot = c * 4 + z
-    my_rows = pl.ds(pl.multiple_of(slot * 16, 16), 16)
-    gsend[0, :16] = jnp.dot(pt[my_rows, :], p_full, preferred_element_type=F32)
-    gsend[0, 16:] = sq[...]
-    gx = [send(gsend.at[0], gxr.at[d - 1], gxs.at[d - 1], gxq.at[d - 1], (at_xy(d, 0), r)) for d in (1, 2, 3)]
-
-    s1 = [add_core(0)]
-    multiply(2)
-    s1 += [add_core(1), add_core(2)]
+    for j in range(4):
+        multiply(0, [(j, k) for k in range(4)])
+    for d in FAR:
+        swap(0, d)
+    for d in FAR:
+        multiply(1, [(mod4(x + d), k) for k in range(4)])
+        swap(1, d)
+    for d in FAR:
+        multiply(2, [(k, mod4(y + d)) for k in range(4)])
+        swap(2, d)
+        add_core(0, d)
+
+    for part in (1, 2):
+        for d in FAR:
+            add_core(part, d)
+    add_line(0)
     for copy in gx:
         copy.wait_recv()
-    gsend[1] = gsend[0] + gxr[0] + gxr[1] + gxr[2]
-    gy1 = [send(gsend.at[1], gyr.at[d - 1], gys.at[d - 1], gyq.at[d - 1], (at_xy(0, d), r)) for d in (1, 2, 3)]
-    add_line(0)
-    for copy in gy1:
-        copy.wait_recv()
-    gmat[slot] = gsend[1] + gyr[0] + gyr[1] + gyr[2]
+    gsum = gsend[0]
+    for k in range(15):
+        gsum = gsum + gxr[k]
+    gmat[slot] = gsum
     g2 = [send(gmat.at[slot], gmat.at[slot], g2s.at[d - 1], g2r.at[d - 1], (f, at_z(d))) for d in (1, 2, 3)]
     add_line(1)
     add_line(2)
@@ -357,26 +372,41 @@
     aug[:, RANK:] = jnp.where(rows_i == cols_i, 1.0, 0.0).astype(F32)
     sub = lax.broadcasted_iota(jnp.int32, (8, 128), 0)
 
+    def spread_row(v, i):
+        return jnp.broadcast_to(v[i : i + 1, :], (8, 128))
+
     def panel(k, _):
-        base = pl.multiple_of(k * 8, 8)
-        rowp = aug[pl.ds(base, 8), :RANK]
-        ext = aug[pl.ds(base, 8), RANK:]
-        turned = pltpu.roll(rowp, lax.rem(128 - base, 128), 1)
-        col = [jnp.broadcast_to(turned[:, j : j + 1], (8, 128)) for j in range(8)]
-        for j in range(8):
-            pivot = jnp.broadcast_to(col[j][j : j + 1, :], (8, 128))
-            inv = lax.rsqrt(pivot)
-            inv = inv * (1.5 - 0.5 * pivot * inv * inv)
-            low = jnp.where(sub > j, col[j] * inv, 0.0)
-            for m in range(j + 1, 8):
-                col[m] = col[m] - low * jnp.broadcast_to(low[m : m + 1, :], (8, 128))
-            row_r = jnp.broadcast_to(rowp[j : j + 1, :], (8, 128)) * inv
-            row_e = jnp.broadcast_to(ext[j : j + 1, :], (8, 128)) * inv
-            rowp = jnp.where(sub == j, row_r, rowp - low * row_r)
-            ext = jnp.where(sub == j, row_e, ext - low * row_e)
-        wbuf[pl.ds(base, 8), :] = ext
-        v1, v2, v3 = split3(rowp)
-        e1, e2, e3 = split3(ext)
+        base = pl.multiple_of(k * 16, 16)
+        halves = (pl.ds(base, 8), pl.ds(base + 8, 8))
+        rowp = [aug[at, :RANK] for at in halves]
+        ext = [aug[at, RANK:] for at in halves]
+        turned = [pltpu.roll(v, lax.rem(128 - base, 128), 1) for v in rowp]
+        col = [[jnp.broadcast_to(v[:, j : j + 1], (8, 128)) for v in turned] for j in range(16)]
+        diag = [jnp.ones((8, 128), F32)] * 2
+        for j in range(16):
+            top, i = j // 8, j % 8
+            pivot = spread_row(col[j][top], i)
+            inv = 1.0 / pivot
+            low = [None, None]
+            for h in range(top, 2):
+                low[h] = col[j][h] * inv
+            low[top] = jnp.where(sub > i, low[top], 0.0)
+            pivots = [spread_row(col[m][top], i) for m in range(j + 1, 16)]
+            row_r, row_e = spread_row(rowp[top], i), spread_row(ext[top], i)
+            for h in range(top, 2):
+                for m in range(j + 1, 16):
+                    col[m][h] = col[m][h] - low[h] * pivots[m - j - 1]
+                rowp[h] = rowp[h] - low[h] * row_r
+                ext[h] = ext[h] - low[h] * row_e
+            diag[top] = jnp.where(sub == i, pivot, diag[top])
+        for h in (0, 1):
+            inv = lax.rsqrt(diag[h])
+            inv = inv * (1.5 - 0.5 * diag[h] * inv * inv)
+            rowp[h] = rowp[h] * inv
+            ext[h] = ext[h] * inv
+            wbuf[halves[h], :] = ext[h]
+        v1, v2, v3 = split3(jnp.concatenate(rowp, axis=0))
+        e1, e2, e3 = split3(jnp.concatenate(ext, axis=0))
         left = jnp.concatenate([v1, v1, v2, v2, v1, v3], axis=0).T.astype(BF16)
         top = jnp.concatenate([v1, v2, v1, v2, v3, v1], axis=0)
         more = jnp.concatenate([e1, e2, e1, e2, e3, e1], axis=0)
@@ -396,18 +426,21 @@
         ])
         passed.append([send(here, here, fs.at[part, 0], fr.at[part, 0], sibling)])
 
-    lax.fori_loop(0, 9, panel, 0)
-    for part in range(3):
-        spread(part)
+    lax.fori_loop(0, 5, panel, 0)
+    spread(0)
+    lax.fori_loop(5, 6, panel, 0)
+    spread(1)
+    lax.fori_loop(6, 7, panel, 0)
+    spread(2)
     for group_of in s1:
         sent += group_of
-    for copy in sent + gx + gy1 + g2 + [g3] + core:
+    for copy in sent + gx + g2 + [g3] + list(core.values()):
         copy.wait_send()
     for part in range(3):
         region = rs2.at[part]
         for sems in (r2s, a1s):
             describe(region, region, sems.at[part], r2r.at[part], sibling).wait_send()
-    lax.fori_loop(9, 16, panel, 0)
+    lax.fori_loop(7, 8, panel, 0)
 
     w = wbuf[...]
     pb = jnp.zeros((ROWS, RANK), F32)
@@ -514,7 +547,7 @@
             vmem((8, PIECE, RANK), BF16),
             vmem((RANK, ROWS), BF16),
             vmem((2, 24, RANK), F32),
-            vmem((3, 24, RANK), F32),
+            vmem((15, 24, RANK), F32),
             vmem((3, 24, RANK), F32),
             vmem((8, 24, RANK), F32),
             vmem((RANK, 2 * RANK), F32),
@@ -539,16 +572,16 @@
             dma((7,)),
             dma((7,)),
             dma((7,)),
-            dma((3,)),
-            dma((3,)),
+            dma((15,)),
+            dma((15,)),
             dma((3,)),
             dma((3,)),
             dma((3,)),
             dma((3,)),
             dma((1,)),
             dma((1,)),
-            dma((3,)),
-            dma((3,)),
+            dma((3, 4)),
+            dma((3, 4)),
             dma((3, 3)),
             dma((3, 3)),
             dma((3, 3)),

time: 62.7 us -> 60.5 us (0.965)
  Pallas kernels: 60.3 us -> 58.2 us
    pallas_call x1, Pallas kernels: 57.9 us -> 55.8 us  [body(): pl.pallas_call(exchange, out_shape=(jax.ShapeDtypeStruct((ROWS, D), BF16)...]
where the time goes in v5:
time: 60.5 us; the launch traced here: 60.4 us
  Pallas kernels  58.2 us (96%)
  between operations  1.29 us (2%)
  local copies, waits for them, and re-layouts  0.92 us (2%)
    pallas_call x1, Pallas kernels, body(): pl.pallas_call(exchange, out_shape=(jax.ShapeDtypeStruct((ROWS, D), BF16)...  55.8 us
    pallas_call x1, Pallas kernels, body(): pl.pallas_call(hand_over, out_shape=(jax.ShapeDtypeStruct((ROWS, D), BF16...  2.39 us

profile of v5, /device:TPU:1, one launch (start us, length us, event | category | flops | bytes accessed | tf_op | source)
XLA Modules:
  0.0 60.4 jit_solution(12007918776660446755)
XLA Ops:
  1.3 0.0 copy-start
  1.3 0.9 %copy-done = f32[384,128]{1,0:T(8,128)S(1)} copy-done((f32[384,128]{1,0:T(8,128)S(1)}, f32[384,128]{1,0:T(8,128)}, u32[]{:S(2)}) %copy-start) | copy-done | bytes 196632
  2.2 55.8 %exchange.1 = (bf16[384,6144]{1,0:T(8,128)(2,1)S(1)}, f32[384,128]{1,0:T(8,128)S(1)}, f32[384,128]{1,0:T(8,128)S(1)}) custom-call(f32[1,1]{1,0:T(1,128)} %bitcast.4.clip_ref, bf16[384,6144]{1,0:T(8,128)(2,1)} %bitcast.5, bf16[384,6144]{1,0:T(8,128)(2,1)} %bitcast.6, f32[384,128]{1,0:T(8,128)S(1)} %copy-done), custom_call_target="tpu_custom_call" | custom-call | tf_op jit(solution)/shard_map/exchange/pallas_call | solution.py:529
  58.0 2.4 %hand_over.1 = (bf16[384,6144]{1,0:T(8,128)(2,1)}, f32[384,128]{1,0:T(8,128)}, f32[384,128]{1,0:T(8,128)}) custom-call(bf16[384,6144]{1,0:T(8,128)(2,1)S(1)} %get-tuple-element.9.new_ref, f32[384,128]{1,0:T(8,128)S(1)} %get-tuple-element.10.basis_ref, f32[384,128]{1,0:T(8,128)S(1)} %get-tuple-element.11.q_ref), custom_call_target="tpu_custom_call" | custom-call | tf_op jit(solution)/shard_map/hand_over/pallas_call | solution.py:602
Async XLA Ops:
  1.3 0.9 %copy-start = (f32[384,128]{1,0:T(8,128)S(1)}, f32[384,128]{1,0:T(8,128)}, u32[]{:S(2)}) copy-start(f32[384,128]{1,0:T(8,128)} %q_ref.1) | copy-start | bytes 589828

commit v6 on v5

--- a/solution.py
+++ b/solution.py
@@ -15,7 +15,6 @@
 CHUNKS = 8
 CHUNK = ROWS // CHUNKS
 HALF = ROWS // 2
-PIECE = ROWS // 8
 FAR = (2, 1, 3, 0)
 PLANE = [(d, e) for d in FAR for e in FAR][:-1]
 
@@ -48,8 +47,8 @@
     qh,
     pacc,
     sq,
-    psend,
-    precv,
+    phalf,
+    pz,
     pall,
     pt,
     gsend,
@@ -78,6 +77,8 @@
     p1r,
     p2s,
     p2r,
+    p3s,
+    p3r,
     gxs,
     gxq,
     gys,
@@ -104,11 +105,15 @@
     x, y, z, c = f // 4, lax.rem(f, 4), r // 2, lax.rem(r, 2)
     sibling = (f, z * 2 + 1 - c)
 
+    xs = [mod4(x + d) * 4 for d in range(4)]
+    ys = [mod4(y + d) for d in range(4)]
+    zs = [mod4(z + d) * 2 + c for d in range(4)]
+
     def at_xy(dx, dy):
-        return mod4(x + dx) * 4 + mod4(y + dy)
+        return xs[dx] + ys[dy]
 
     def at_z(dz):
-        return mod4(z + dz) * 2 + c
+        return zs[dz]
 
     def describe(src, dst, ssem, rsem, device):
         return pltpu.make_async_remote_copy(
@@ -126,20 +131,19 @@
     qload.start()
 
     barrier = pltpu.get_barrier_semaphore()
-    peers = [sibling]
-    for d in (1, 2, 3):
-        peers += [(at_xy(d, 0), r), (at_xy(0, d), r), (f, at_z(d)), (f, mod4(z + d) * 2 + 1 - c)]
+    peers = []
+    for d in (2, 1, 3):
+        peers += [(at_xy(d, 0), r), (at_xy(0, d), r)]
+    peers.append(sibling)
+    for d in (2, 1, 3):
+        peers.append((f, at_z(d)))
     for device in peers:
         pl.semaphore_signal(barrier, inc=1, device_id=device, device_id_type=MESH)
 
-    loads = []
     for k in range(CHUNKS):
         rows = pl.ds(k * CHUNK, CHUNK)
-        a = pltpu.make_async_copy(grads.at[rows], gbuf.at[rows], load_sem.at[0, k])
-        b = pltpu.make_async_copy(errors.at[rows], ebuf.at[rows], load_sem.at[1, k])
-        a.start()
-        b.start()
-        loads.append((a, b))
+        pltpu.make_async_copy(grads.at[rows], gbuf.at[rows], load_sem.at[0, k]).start()
+        pltpu.make_async_copy(errors.at[rows], ebuf.at[rows], load_sem.at[1, k]).start()
 
     s_me, t_me = jnp.where(c == 0, y, x), jnp.where(c == 0, x, y)
     qload.wait()
@@ -163,10 +167,10 @@
     q2 = [send(own, own, q2s.at[0, d - 1], q2r.at[d - 1], along_s(d)) for d in (1, 2, 3)]
     q3 = [send(own, own, q3s.at[0], q3r.at[0], sibling)]
 
-    def merge(k):
-        a, b = loads[k]
-        a.wait()
-        b.wait()
+    def merge(k, _):
+        rows = pl.ds(pl.multiple_of(k * CHUNK, CHUNK), CHUNK)
+        pltpu.make_async_copy(grads.at[rows], gbuf.at[rows], load_sem.at[0, k]).wait()
+        pltpu.make_async_copy(errors.at[rows], ebuf.at[rows], load_sem.at[1, k]).wait()
 
         def group(i, _):
             rows = pl.ds(pl.multiple_of(k * CHUNK + i * 16, 16), 16)
@@ -182,82 +186,63 @@
             return 0
 
         lax.fori_loop(0, CHUNK // 16, group, 0)
-
-    for k in range(3):
-        merge(k)
+        return 0
+
+    lax.fori_loop(0, 3, merge, 0)
     for d in (1, 3, 2):
         q1[d - 1].wait_recv()
         here = qh.at[c, s_me, mod4(t_me - d), filled]
         for e in (2, 1, 3):
             q2.append(send(here, here, q2s.at[d, e - 1], q2r.at[e - 1], along_s(e)))
         q3.append(send(here, here, q3s.at[d], q3r.at[d], sibling))
-    for k in range(3, CHUNKS):
-        merge(k)
-    def add_p(half, s, first=False):
-        cols = []
-        for t in range(4):
-            g = jnp.where(half == 0, t * 4 + s, s * 4 + t)
-            cols.append(gbuf[:, pl.ds(pl.multiple_of(g * ROWS + half * 128, 128), 256)])
+    lax.fori_loop(3, CHUNKS, merge, 0)
+    def add_p(half, places, first=False):
+        cols, right = [], []
+        for s in places:
+            right.append(qh[half, s].reshape(1024, RANK))
+            for t in range(4):
+                g = jnp.where(half == 0, t * 4 + s, s * 4 + t)
+                cols.append(gbuf[:, pl.ds(pl.multiple_of(g * ROWS + half * 128, 128), 256)])
         term = jnp.dot(
-            jnp.concatenate(cols, axis=1), qh[half, s].reshape(1024, RANK), preferred_element_type=F32
+            jnp.concatenate(cols, axis=1), jnp.concatenate(right, axis=0), preferred_element_type=F32
         )
         if first:
             pacc[...] = term
         else:
             pacc[...] += term
 
-    def pass_q(d):
+    add_p(c, [s_me], True)
+    for copy in q3[:4]:
+        copy.wait_recv()
+    add_p(1 - c, [t_me])
+    for d in (1, 3, 2):
         here = qh.at[c, mod4(s_me - d), :, filled]
         describe(here, here, q2s.at[0, 0], q2r.at[d - 1], sibling).wait_recv()
         q3.append(send(here, here, q3s.at[3 + d], q3r.at[3 + d], sibling))
-        add_p(c, mod4(s_me - d))
-
-    add_p(c, s_me, True)
-    pass_q(1)
-    for copy in q3[:4]:
+    add_p(c, [mod4(s_me - d) for d in (1, 3, 2)])
+    for copy in q3[4:]:
         copy.wait_recv()
-    add_p(1 - c, t_me)
-    pass_q(3)
-    q3[4].wait_recv()
-    add_p(1 - c, mod4(t_me - 1))
-    pass_q(2)
-    q3[5].wait_recv()
-    add_p(1 - c, mod4(t_me - 3))
-    q3[6].wait_recv()
-    add_p(1 - c, mod4(t_me - 2))
+    add_p(1 - c, [mod4(t_me - d) for d in (1, 3, 2)])
     sent += q1 + q2 + q3
 
-    for k in range(8):
-        psend[k] = pacc[k * PIECE : (k + 1) * PIECE].astype(BF16)
-    p1 = []
-    for e in (4, 3, 5, 2, 6, 1, 7):
-        other = lax.rem(r + e, 8)
-        p1.append(send(psend.at[other], precv.at[r], p1s.at[e - 1], p1r.at[e - 1], (f, other)))
-    precv[r] = psend[r]
-    for copy in p1:
-        copy.wait_recv()
-    total = precv[0].astype(F32)
-    for k in range(1, 8):
-        total = total + precv[k].astype(F32)
-    pall[r] = total.astype(BF16)
-    p2 = []
-    for e in (4, 3, 5, 2, 6, 1, 7):
-        other = lax.rem(r + e, 8)
-        p2.append(send(pall.at[r], pall.at[r], p2s.at[e - 1], p2r.at[e - 1], (f, other)))
+    half_c = pl.ds(pl.multiple_of(c * HALF, HALF), HALF)
+    other_half = pl.ds(pl.multiple_of((1 - c) * HALF, HALF), HALF)
+    p1 = send(pacc.at[other_half], phalf, p1s, p1r, sibling)
+    p1.wait_recv()
+    pz[z] = (pacc[half_c, :] + phalf[...]).astype(BF16)
+    p2 = [send(pz.at[z], pz.at[z], p2s.at[d - 1], p2r.at[d - 1], (f, at_z(d))) for d in (2, 1, 3)]
     for copy in p2:
         copy.wait_recv()
-    sent += p1 + p2
+    total = pz[0].astype(F32)
+    for k in range(1, 4):
+        total = total + pz[k].astype(F32)
+    pall[c] = total.astype(BF16)
+    p3 = send(pall.at[c], pall.at[c], p3s, p3r, sibling)
+    p3.wait_recv()
+    sent += [p1, p3] + p2
 
     p_full = pall[...].reshape(ROWS, RANK)
     pt[...] = p_full.T
-
-    slot = c * 4 + z
-    my_rows = pl.ds(pl.multiple_of(slot * 16, 16), 16)
-    gsend[0, :16] = jnp.dot(pt[my_rows, :], p_full, preferred_element_type=F32)
-    gsend[0, 16:] = sq[...]
-    gx = [
-        send(gsend.at[0], gxr.at[k], gxs.at[k], gxq.at[k], (at_xy(dx, dy), r)) for k, (dx, dy) in enumerate(PLANE)
-    ]
 
     core, s1 = {}, ([], [], [])
     order = ((z, x, y), (x, y, z), (y, z, x))
@@ -336,17 +321,26 @@
         multiply(0, [(j, k) for k in range(4)])
     for d in FAR:
         swap(0, d)
+
+    slot = c * 4 + z
+    my_rows = pl.ds(pl.multiple_of(slot * 16, 16), 16)
+    gsend[0, :16] = jnp.dot(pt[my_rows, :], p_full, preferred_element_type=F32)
+    gsend[0, 16:] = sq[...]
+    gx = [
+        send(gsend.at[0], gxr.at[k], gxs.at[k], gxq.at[k], (at_xy(dx, dy), r)) for k, (dx, dy) in enumerate(PLANE)
+    ]
+
     for d in FAR:
         multiply(1, [(mod4(x + d), k) for k in range(4)])
         swap(1, d)
+        add_core(0, d)
     for d in FAR:
         multiply(2, [(k, mod4(y + d)) for k in range(4)])
         swap(2, d)
-        add_core(0, d)
-
-    for part in (1, 2):
-        for d in FAR:
-            add_core(part, d)
+        add_core(1, d)
+    for d in FAR:
+        add_core(2, d)
+
     add_line(0)
     for copy in gx:
         copy.wait_recv()
@@ -426,11 +420,11 @@
         ])
         passed.append([send(here, here, fs.at[part, 0], fr.at[part, 0], sibling)])
 
-    lax.fori_loop(0, 5, panel, 0)
+    lax.fori_loop(0, 3, panel, 0)
     spread(0)
-    lax.fori_loop(5, 6, panel, 0)
+    lax.fori_loop(3, 4, panel, 0)
     spread(1)
-    lax.fori_loop(6, 7, panel, 0)
+    lax.fori_loop(4, 5, panel, 0)
     spread(2)
     for group_of in s1:
         sent += group_of
@@ -440,7 +434,8 @@
         region = rs2.at[part]
         for sems in (r2s, a1s):
             describe(region, region, sems.at[part], r2r.at[part], sibling).wait_send()
-    lax.fori_loop(7, 8, panel, 0)
+
+    lax.fori_loop(5, 8, panel, 0)
 
     w = wbuf[...]
     pb = jnp.zeros((ROWS, RANK), F32)
@@ -529,9 +524,9 @@
     new_errors, basis, q_out = pl.pallas_call(
         exchange,
         out_shape=(
-            jax.ShapeDtypeStruct((ROWS, D), BF16),
-            jax.ShapeDtypeStruct((ROWS, RANK), F32),
-            jax.ShapeDtypeStruct((ROWS, RANK), F32),
+            vmem((ROWS, D), BF16),
+            vmem((ROWS, RANK), F32),
+            vmem((ROWS, RANK), F32),
         ),
         in_specs=[pl.BlockSpec(memory_space=pltpu.SMEM), hbm, hbm, hbm],
         out_specs=(inside, inside, inside),
@@ -542,9 +537,9 @@
             vmem((2, 4, 4, 256, RANK), BF16),
             vmem((ROWS, RANK), F32),
             vmem((8, 128), F32),
-            vmem((8, PIECE, RANK), BF16),
-            vmem((8, PIECE, RANK), BF16),
-            vmem((8, PIECE, RANK), BF16),
+            vmem((HALF, RANK), F32),
+            vmem((4, HALF, RANK), BF16),
+            vmem((2, HALF, RANK), BF16),
             vmem((RANK, ROWS), BF16),
             vmem((2, 24, RANK), F32),
             vmem((15, 24, RANK), F32),
@@ -568,10 +563,12 @@
             dma((3,)),
             dma((7,)),
             dma((7,)),
-            dma((7,)),
-            dma((7,)),
-            dma((7,)),
-            dma((7,)),
+            dma(()),
+            dma(()),
+            dma((3,)),
+            dma((3,)),
+            dma(()),
+            dma(()),
             dma((15,)),
             dma((15,)),
             dma((3,)),
@@ -594,10 +591,10 @@
             dma((3, 4)),
         ],
         compiler_params=pltpu.CompilerParams(
-            collective_id=0, has_side_effects=True, vmem_limit_bytes=47 * 1024 * 1024
+            collective_id=0, has_side_effects=True, vmem_limit_bytes=40 * 1024 * 1024
         ),
         name="exchange",
-    )(clip_rms.reshape(1, 1), grads[0], errors[0], q_start)
+    )(clip_rms.reshape(1, 1), *[pltpu.with_memory_space_constraint(v, pltpu.HBM) for v in (grads[0], errors[0], q_start)])
     anywhere = pl.BlockSpec(memory_space=pl.ANY)
     new_errors, basis, q_out = pl.pallas_call(
         hand_over,

time: 60.5 us -> 59.1 us (0.977)
  local copies, waits for them, and re-layouts: 0.92 us -> 0 us
    unnamed x2 -> x0, local copies, waits for them, and re-layouts: 0.92 us -> none
where the time goes in v6:
time: 59.1 us; the launch traced here: 59 us
  Pallas kernels  57.7 us (98%)
  between operations  1.29 us (2%)
    pallas_call x1, Pallas kernels, body(): pl.pallas_call(exchange, out_shape=(vmem((ROWS, D), BF16), vmem((ROWS, RA...  55.3 us
    pallas_call x1, Pallas kernels, body(): pl.pallas_call(hand_over, out_shape=(jax.ShapeDtypeStruct((ROWS, D), BF16...  2.39 us

profile of v6, /device:TPU:1, one launch (start us, length us, event | category | flops | bytes accessed | tf_op | source)
XLA Modules:
  0.0 59.0 jit_solution(2390458247695134422)
XLA Ops:
  1.3 55.3 %exchange.1 = (bf16[384,6144]{1,0:T(8,128)(2,1)S(1)}, f32[384,128]{1,0:T(8,128)S(1)}, f32[384,128]{1,0:T(8,128)S(1)}) custom-call(f32[1,1]{1,0:T(1,128)} %bitcast.4.clip_ref, bf16[384,6144]{1,0:T(8,128)(2,1)} %bitcast.5, bf16[384,6144]{1,0:T(8,128)(2,1)} %bitcast.6, f32[384,128]{1,0:T(8,128)} %q_ref.1), custom_call_target="tpu_custom_call" | custom-call | tf_op jit(solution)/shard_map/exchange/pallas_call | solution.py:524
  56.6 2.4 %hand_over.1 = (bf16[384,6144]{1,0:T(8,128)(2,1)}, f32[384,128]{1,0:T(8,128)}, f32[384,128]{1,0:T(8,128)}) custom-call(bf16[384,6144]{1,0:T(8,128)(2,1)S(1)} %get-tuple-element.9.new_ref, f32[384,128]{1,0:T(8,128)S(1)} %get-tuple-element.10.basis_ref, f32[384,128]{1,0:T(8,128)S(1)} %get-tuple-element.11.q_ref), custom_call_target="tpu_custom_call" | custom-call | tf_op jit(solution)/shard_map/hand_over/pallas_call | solution.py:599

commit v7 on v6

--- a/solution.py
+++ b/solution.py
@@ -38,10 +38,11 @@
     grads,
     errors,
     q_ref,
-    new_ref,
+    gbuf,
+    gy,
+    bmat,
     basis_ref,
-    qout_ref,
-    gbuf,
+    w_ref,
     ebuf,
     qin,
     qh,
@@ -57,14 +58,12 @@
     gmat,
     aug,
     wbuf,
-    bmat,
     yl,
     yr,
     yc,
     rs1,
     t1,
     rs2,
-    gy,
     load_sem,
     qin_sem,
     q1s,
@@ -315,7 +314,7 @@
         gy[c, part, mine] = value.astype(BF16)
         here = gy.at[c, part, mine]
         for d, e in PLANE:
-            send(here, here, a1s.at[part], a1r.at[part], way(part, (0, d, e)))
+            send(here, here, a1s.at[part], a1r.at[part, d], way(part, (0, d, e)))
 
     for j in range(4):
         multiply(0, [(j, k) for k in range(4)])
@@ -411,14 +410,17 @@
     lines, passed = [], []
 
     def spread(part):
-        a0 = order[part][0]
+        a0, a1, _ = order[part]
+        for d in FAR:
+            region = rs2.at[part, pl.ds(0, 4 if d else 3)]
+            describe(region, region, a1s.at[part], a1r.at[part, d], sibling).wait_recv()
+            here = gy.at[c, part, pl.ds(a0 * 16 + mod4(a1 - d) * 4, 4)]
+            for e in (2, 1, 3):
+                send(here, here, a2s.at[part, e - 1], a2r.at[part, e - 1], way(part, (e, 0, 0)))
+            send(here, here, fs.at[part, 0], fr.at[part, 0], sibling)
         here = gy.at[c, part, pl.ds(a0 * 16, 16)]
-        region = rs2.at[part]
-        describe(region, region, a1s.at[part], a1r.at[part], sibling).wait_recv()
-        lines.append([
-            send(here, here, a2s.at[part, d - 1], a2r.at[part, d - 1], way(part, (d, 0, 0))) for d in (1, 2, 3)
-        ])
-        passed.append([send(here, here, fs.at[part, 0], fr.at[part, 0], sibling)])
+        lines.append([describe(here, here, a2s.at[part, e], a2r.at[part, e], sibling) for e in range(3)])
+        passed.append([describe(here, here, fs.at[part, 0], fr.at[part, 0], sibling)])
 
     lax.fori_loop(0, 3, panel, 0)
     spread(0)
@@ -449,69 +451,48 @@
         jnp.dot(pb, w, preferred_element_type=F32, precision=lax.Precision.HIGHEST) * 0.125
     ).astype(BF16)
 
-    def right(part, x2, y2):
-        tiles = [gy[c2, part, tile_of(part, x2, y2, z2)] for c2 in (0, 1) for z2 in range(4)]
-        return jnp.concatenate(tiles, axis=0)
-
-    def update(part, places):
-        low = jnp.dot(
-            bmat[...],
-            jnp.concatenate([right(part, x2, y2) for x2, y2 in places], axis=1),
-            preferred_element_type=F32,
-        )
-        for k, (x2, y2) in enumerate(places):
-            cols = pl.ds(pl.multiple_of((x2 * 4 + y2) * ROWS + part * 128, 128), 128)
-            new_ref[:, cols] = (gbuf[:, cols].astype(F32) - low[:, k * 128 : (k + 1) * 128]).astype(BF16)
-
-    def pass_line(d):
+    squares = jnp.sum(jnp.sum(gmat[:, 16:], axis=0))
+    root_mean = jnp.sqrt(jnp.full((1, RANK), squares) / (8 * D * D) + 1e-06)
+    w_ref[...] = wbuf[...] * (jnp.minimum(1.0, clip_ref[0, 0] / root_mean) * 0.125)
+
+    for d in (1, 3, 2):
         for part in range(3):
             lines[part][d - 1].wait_recv()
             here = gy.at[c, part, pl.ds(mod4(order[part][0] - d) * 16, 16)]
             passed[part].append(send(here, here, fs.at[part, d], fr.at[part, d], sibling))
-
-    def groups(d):
-        for part in range(3):
-            passed[part][(0, 1, 3, 2)[d]].wait_recv()
-            a0 = mod4(order[part][0] - d)
-            if part == 1:
-                update(part, [(a0, k) for k in range(4)])
-            if part == 2:
-                update(part, [(k, a0) for k in range(4)])
-
-    groups(0)
-    pass_line(1)
-    pass_line(3)
-    groups(1)
-    pass_line(2)
-    groups(3)
-    groups(2)
-    for j in range(4):
-        update(0, [(j, k) for k in range(4)])
-
-    squares = jnp.sum(jnp.sum(gmat[:, 16:], axis=0))
-    root_mean = jnp.sqrt(jnp.full((1, RANK), squares) / (8 * D * D) + 1e-06)
-    scale = jnp.minimum(1.0, clip_ref[0, 0] / root_mean) * 0.125
-    block = jnp.concatenate([right(part, x, y) for part in range(3)], axis=1)
-    value = jnp.zeros((RANK, ROWS), F32)
-    for piece in split3(wbuf[...])[::-1]:
-        value = value + jnp.dot(piece.astype(BF16), block, preferred_element_type=F32)
-    qout_ref[...] = value.T * scale
-
+    for group_of in passed:
+        for copy in group_of:
+            copy.wait_recv()
     for group_of in lines + passed:
         for copy in group_of:
             copy.wait_send()
 
 
-def hand_over(new_ref, basis_ref, q_ref, new_out, basis_out, q_out, sems):
-    copies = [
-        pltpu.make_async_copy(basis_ref, basis_out, sems.at[CHUNKS]),
-        pltpu.make_async_copy(q_ref, q_out, sems.at[CHUNKS + 1]),
-    ]
-    for k in range(CHUNKS):
-        rows = pl.ds(k * CHUNK, CHUNK)
-        copies.append(pltpu.make_async_copy(new_ref.at[rows], new_out.at[rows], sems.at[k]))
-    for copy in copies:
-        copy.start()
+def update(merged, gy, bmat, basis, w_ref, new_out, basis_out, q_out, new, q_buf, sems):
+    f = lax.axis_index("fsdp")
+    x, y = f // 4, lax.rem(f, 4)
+
+    def right(part, x2, y2):
+        tiles = [gy[c2, part, tile_of(part, x2, y2, z2)] for c2 in (0, 1) for z2 in range(4)]
+        return jnp.concatenate(tiles, axis=0)
+
+    copies = [pltpu.make_async_copy(basis, basis_out, sems.at[CHUNKS])]
+    copies[0].start()
+    for j in range(CHUNKS):
+        cols = pl.ds(j * 768, 768)
+        places = [((2 * j + k) // 4, (2 * j + k) % 4) for k in (0, 1)]
+        block = jnp.concatenate([right(part, x2, y2) for x2, y2 in places for part in range(3)], axis=1)
+        low = jnp.dot(bmat[...], block, preferred_element_type=F32)
+        new[:, cols] = (merged[:, cols].astype(F32) - low).astype(BF16)
+        copies.append(pltpu.make_async_copy(new.at[:, cols], new_out.at[:, cols], sems.at[j]))
+        copies[-1].start()
+    block = jnp.concatenate([right(part, x, y) for part in range(3)], axis=1)
+    value = jnp.zeros((RANK, ROWS), F32)
+    for piece in split3(w_ref[...])[::-1]:
+        value = value + jnp.dot(piece.astype(BF16), block, preferred_element_type=F32)
+    q_buf[...] = value.T
+    copies.append(pltpu.make_async_copy(q_buf, q_out, sems.at[CHUNKS + 1]))
+    copies[-1].start()
     for copy in copies:
         copy.wait()
 
@@ -521,17 +502,18 @@
     vmem = pltpu.VMEM
     hbm = pl.BlockSpec(memory_space=pltpu.HBM)
     inside = pl.BlockSpec(memory_space=pltpu.VMEM)
-    new_errors, basis, q_out = pl.pallas_call(
+    merged, gy, bmat, basis, w = pl.pallas_call(
         exchange,
         out_shape=(
             vmem((ROWS, D), BF16),
+            vmem((2, 3, 64, 16, 128), BF16),
+            vmem((ROWS, RANK), BF16),
             vmem((ROWS, RANK), F32),
-            vmem((ROWS, RANK), F32),
+            vmem((RANK, RANK), F32),
         ),
         in_specs=[pl.BlockSpec(memory_space=pltpu.SMEM), hbm, hbm, hbm],
-        out_specs=(inside, inside, inside),
+        out_specs=(inside,) * 5,
         scratch_shapes=[
-            vmem((ROWS, D), BF16),
             vmem((ROWS, D), BF16),
             vmem((HALF, RANK), F32),
             vmem((2, 4, 4, 256, RANK), BF16),
@@ -547,14 +529,12 @@
             vmem((8, 24, RANK), F32),
             vmem((RANK, 2 * RANK), F32),
             vmem((RANK, RANK), F32),
-            vmem((ROWS, RANK), BF16),
             vmem((2, 3, 64, 16, 128), BF16),
             vmem((3, 64, 16, 128), BF16),
             vmem((3, 64, 16, 128), BF16),
             vmem((3, 3, 16, 16, 128), BF16),
             vmem((3, 16, 16, 128), BF16),
             vmem((3, 15, 16, 128), BF16),
-            vmem((2, 3, 64, 16, 128), BF16),
             dma((2, CHUNKS)),
             dma(()),
             dma((3,)),
@@ -586,7 +566,7 @@
             dma((3,)),
             dma((3,)),
             dma((3,)),
-            dma((3,)),
+            dma((3, 4)),
             dma((3, 4)),
             dma((3, 4)),
         ],
@@ -595,20 +575,19 @@
         ),
         name="exchange",
     )(clip_rms.reshape(1, 1), *[pltpu.with_memory_space_constraint(v, pltpu.HBM) for v in (grads[0], errors[0], q_start)])
-    anywhere = pl.BlockSpec(memory_space=pl.ANY)
     new_errors, basis, q_out = pl.pallas_call(
-        hand_over,
+        update,
         out_shape=(
             jax.ShapeDtypeStruct((ROWS, D), BF16),
             jax.ShapeDtypeStruct((ROWS, RANK), F32),
             jax.ShapeDtypeStruct((ROWS, RANK), F32),
         ),
-        in_specs=[anywhere] * 3,
-        out_specs=(anywhere,) * 3,
-        scratch_shapes=[dma((CHUNKS + 2,))],
-        compiler_params=pltpu.CompilerParams(vmem_limit_bytes=1024 * 1024),
-        name="hand_over",
-    )(new_errors, basis, q_out)
+        in_specs=[inside] * 5,
+        out_specs=(pl.BlockSpec(memory_space=pl.ANY),) * 3,
+        scratch_shapes=[vmem((ROWS, D), BF16), vmem((ROWS, RANK), F32), dma((CHUNKS + 2,))],
+        compiler_params=pltpu.CompilerParams(vmem_limit_bytes=24 * 1024 * 1024),
+        name="update",
+    )(*[pltpu.with_memory_space_constraint(v, pltpu.VMEM) for v in (merged, gy, bmat, basis, w)])
     return new_errors[None], basis, q_out
 
 

time: 59.1 us -> 58.4 us (0.988)
  Pallas kernels: 57.7 us -> 57 us
    pallas_call x2, Pallas kernels: 57.7 us -> 57 us  [the longest x1 54.3 us: body(): pl.pallas_call(exchange, out_shape=(vmem((ROWS, D), BF16), vmem((2, 3, 64...]
where the time goes in v7:
time: 58.4 us; the launch traced here: 58.3 us
  Pallas kernels  57 us (98%)
  between operations  1.29 us (2%)
    pallas_call x1, Pallas kernels, body(): pl.pallas_call(exchange, out_shape=(vmem((ROWS, D), BF16), vmem((2, 3, 64...  54.3 us
    pallas_call x1, Pallas kernels, body(): pl.pallas_call(update, out_shape=(jax.ShapeDtypeStruct((ROWS, D), BF16),...  2.63 us

profile of v7, /device:TPU:1, one launch (start us, length us, event | category | flops | bytes accessed | tf_op | source)
XLA Modules:
  0.0 58.3 jit_solution(17548991867900449289)
XLA Ops:
  1.3 54.3 %exchange.1 = (bf16[384,6144]{1,0:T(8,128)(2,1)S(1)}, bf16[2,3,64,16,128]{4,3,2,1,0:T(8,128)(2,1)S(1)}, bf16[384,128]{1,0:T(8,128)(2,1)S(1)}, f32[384,128]{1,0:T(8,128)S(1)}, f32[128,128]{1,0:T(8,128)S(1)}) custom-call(f32[1,1]{1,0:T(1,128)} %bitcast.4.clip_ref, bf16[384,6144]{1,0:T(8,128)(2,1)} %bitcast.5, bf16[384,6144]{1,0:T(8,128)(2,1)} %bitcast.6, ...), custom_call_target="tpu_custom_call" | custom-call | tf_op jit(solution)/shard_map/exchange/pallas_call | solution.py:505
  55.6 2.6 %update.1 = (bf16[384,6144]{1,0:T(8,128)(2,1)}, f32[384,128]{1,0:T(8,128)}, f32[384,128]{1,0:T(8,128)}) custom-call(bf16[384,6144]{1,0:T(8,128)(2,1)S(1)} %get-tuple-element.11.merged, bf16[2,3,64,16,128]{4,3,2,1,0:T(8,128)(2,1)S(1)} %get-tuple-element.12.gy, bf16[384,128]{1,0:T(8,128)(2,1)S(1)} %get-tuple-element.13.bmat, ...), custom_call_target="tpu_custom_call" | custom-call | tf_op jit(solution)/shard_map/update/pallas_call | solution.py:578

commit v8 on v7

--- a/solution.py
+++ b/solution.py
@@ -243,6 +243,14 @@
     p_full = pall[...].reshape(ROWS, RANK)
     pt[...] = p_full.T
 
+    slot = c * 4 + z
+    my_rows = pl.ds(pl.multiple_of(slot * 16, 16), 16)
+    gsend[0, :16] = jnp.dot(pt[my_rows, :], p_full, preferred_element_type=F32)
+    gsend[0, 16:] = sq[...]
+    gx = [
+        send(gsend.at[0], gxr.at[k], gxs.at[k], gxq.at[k], (at_xy(dx, dy), r)) for k, (dx, dy) in enumerate(PLANE)
+    ]
+
     core, s1 = {}, ([], [], [])
     order = ((z, x, y), (x, y, z), (y, z, x))
 
@@ -321,24 +329,21 @@
     for d in FAR:
         swap(0, d)
 
-    slot = c * 4 + z
-    my_rows = pl.ds(pl.multiple_of(slot * 16, 16), 16)
-    gsend[0, :16] = jnp.dot(pt[my_rows, :], p_full, preferred_element_type=F32)
-    gsend[0, 16:] = sq[...]
-    gx = [
-        send(gsend.at[0], gxr.at[k], gxs.at[k], gxq.at[k], (at_xy(dx, dy), r)) for k, (dx, dy) in enumerate(PLANE)
-    ]
-
-    for d in FAR:
-        multiply(1, [(mod4(x + d), k) for k in range(4)])
-        swap(1, d)
+    def begin(part, d):
+        multiply(part, [(mod4(x + d), k) for k in range(4)] if part == 1 else [(k, mod4(y + d)) for k in range(4)])
+        swap(part, d)
+
+    for d in (2, 1, 3):
+        begin(1, d)
+        begin(2, d)
         add_core(0, d)
-    for d in FAR:
-        multiply(2, [(k, mod4(y + d)) for k in range(4)])
-        swap(2, d)
+    for d in (2, 1, 3):
         add_core(1, d)
-    for d in FAR:
         add_core(2, d)
+    begin(1, 0)
+    begin(2, 0)
+    for part in range(3):
+        add_core(part, 0)
 
     add_line(0)
     for copy in gx:
@@ -428,15 +433,6 @@
     spread(1)
     lax.fori_loop(4, 5, panel, 0)
     spread(2)
-    for group_of in s1:
-        sent += group_of
-    for copy in sent + gx + g2 + [g3] + list(core.values()):
-        copy.wait_send()
-    for part in range(3):
-        region = rs2.at[part]
-        for sems in (r2s, a1s):
-            describe(region, region, sems.at[part], r2r.at[part], sibling).wait_send()
-
     lax.fori_loop(5, 8, panel, 0)
 
     w = wbuf[...]
@@ -450,6 +446,15 @@
     bmat[...] = (
         jnp.dot(pb, w, preferred_element_type=F32, precision=lax.Precision.HIGHEST) * 0.125
     ).astype(BF16)
+
+    for group_of in s1:
+        sent += group_of
+    for copy in sent + gx + g2 + [g3] + list(core.values()):
+        copy.wait_send()
+    for part in range(3):
+        region = rs2.at[part]
+        for sems in (r2s, a1s):
+            describe(region, region, sems.at[part], r2r.at[part], sibling).wait_send()
 
     squares = jnp.sum(jnp.sum(gmat[:, 16:], axis=0))
     root_mean = jnp.sqrt(jnp.full((1, RANK), squares) / (8 * D * D) + 1e-06)

time: 58.4 us -> 57.6 us (0.986)
  Pallas kernels: 57 us -> 56.2 us
    pallas_call x1, Pallas kernels: 54.3 us -> 53.5 us  [body(): pl.pallas_call(exchange, out_shape=(vmem((ROWS, D), BF16), vmem((2, 3, 64...]
where the time goes in v8:
time: 57.6 us; the launch traced here: 57.4 us
  Pallas kernels  56.2 us (98%)
  between operations  1.29 us (2%)
    pallas_call x1, Pallas kernels, body(): pl.pallas_call(exchange, out_shape=(vmem((ROWS, D), BF16), vmem((2, 3, 64...  53.5 us
    pallas_call x1, Pallas kernels, body(): pl.pallas_call(update, out_shape=(jax.ShapeDtypeStruct((ROWS, D), BF16),...  2.63 us

profile of v8, /device:TPU:1, one launch (start us, length us, event | category | flops | bytes accessed | tf_op | source)
XLA Modules:
  0.0 57.4 jit_solution(17324825545312831095)
XLA Ops:
  1.3 53.5 %exchange.1 = (bf16[384,6144]{1,0:T(8,128)(2,1)S(1)}, bf16[2,3,64,16,128]{4,3,2,1,0:T(8,128)(2,1)S(1)}, bf16[384,128]{1,0:T(8,128)(2,1)S(1)}, f32[384,128]{1,0:T(8,128)S(1)}, f32[128,128]{1,0:T(8,128)S(1)}) custom-call(f32[1,1]{1,0:T(1,128)} %bitcast.4.clip_ref, bf16[384,6144]{1,0:T(8,128)(2,1)} %bitcast.5, bf16[384,6144]{1,0:T(8,128)(2,1)} %bitcast.6, ...), custom_call_target="tpu_custom_call" | custom-call | tf_op jit(solution)/shard_map/exchange/pallas_call | solution.py:510
  54.8 2.6 %update.1 = (bf16[384,6144]{1,0:T(8,128)(2,1)}, f32[384,128]{1,0:T(8,128)}, f32[384,128]{1,0:T(8,128)}) custom-call(bf16[384,6144]{1,0:T(8,128)(2,1)S(1)} %get-tuple-element.11.merged, bf16[2,3,64,16,128]{4,3,2,1,0:T(8,128)(2,1)S(1)} %get-tuple-element.12.gy, bf16[384,128]{1,0:T(8,128)(2,1)S(1)} %get-tuple-element.13.bmat, ...), custom_call_target="tpu_custom_call" | custom-call | tf_op jit(solution)/shard_map/update/pallas_call | solution.py:583

commit v9 on v8

--- a/solution.py
+++ b/solution.py
@@ -346,6 +346,8 @@
         add_core(part, 0)
 
     add_line(0)
+    add_line(1)
+    add_line(2)
     for copy in gx:
         copy.wait_recv()
     gsum = gsend[0]
@@ -353,14 +355,13 @@
         gsum = gsum + gxr[k]
     gmat[slot] = gsum
     g2 = [send(gmat.at[slot], gmat.at[slot], g2s.at[d - 1], g2r.at[d - 1], (f, at_z(d))) for d in (1, 2, 3)]
-    add_line(1)
-    add_line(2)
+    add_plane(0)
+    add_plane(1)
     for copy in g2:
         copy.wait_recv()
     side = gmat.at[pl.ds(c * 4, 4)]
     g3 = send(side, side, g3s.at[0], g3r.at[0], sibling)
-    for part in range(3):
-        add_plane(part)
+    add_plane(2)
 
     g3.wait_recv()
     for k in range(8):

time: 57.6 us -> 57.5 us (level)
  no operation moved by 1% of the time
where the time goes in v9:
time: 57.5 us; the launch traced here: 57.4 us
  Pallas kernels  56.1 us (98%)
  between operations  1.29 us (2%)
    pallas_call x1, Pallas kernels, body(): pl.pallas_call(exchange, out_shape=(vmem((ROWS, D), BF16), vmem((2, 3, 64...  53.5 us
    pallas_call x1, Pallas kernels, body(): pl.pallas_call(update, out_shape=(jax.ShapeDtypeStruct((ROWS, D), BF16),...  2.63 us

profile of v9, /device:TPU:1, one launch (start us, length us, event | category | flops | bytes accessed | tf_op | source)
XLA Modules:
  0.0 57.4 jit_solution(1465701360143552089)
XLA Ops:
  1.3 53.5 %exchange.1 = (bf16[384,6144]{1,0:T(8,128)(2,1)S(1)}, bf16[2,3,64,16,128]{4,3,2,1,0:T(8,128)(2,1)S(1)}, bf16[384,128]{1,0:T(8,128)(2,1)S(1)}, f32[384,128]{1,0:T(8,128)S(1)}, f32[128,128]{1,0:T(8,128)S(1)}) custom-call(f32[1,1]{1,0:T(1,128)} %bitcast.4.clip_ref, bf16[384,6144]{1,0:T(8,128)(2,1)} %bitcast.5, bf16[384,6144]{1,0:T(8,128)(2,1)} %bitcast.6, ...), custom_call_target="tpu_custom_call" | custom-call | tf_op jit(solution)/shard_map/exchange/pallas_call | solution.py:511
  54.7 2.6 %update.1 = (bf16[384,6144]{1,0:T(8,128)(2,1)}, f32[384,128]{1,0:T(8,128)}, f32[384,128]{1,0:T(8,128)}) custom-call(bf16[384,6144]{1,0:T(8,128)(2,1)S(1)} %get-tuple-element.11.merged, bf16[2,3,64,16,128]{4,3,2,1,0:T(8,128)(2,1)S(1)} %get-tuple-element.12.gy, bf16[384,128]{1,0:T(8,128)(2,1)S(1)} %get-tuple-element.13.bmat, ...), custom_call_target="tpu_custom_call" | custom-call | tf_op jit(solution)/shard_map/update/pallas_call | solution.py:584
